TPU v7x, 128 devices: a whole 4x4x4 slice. The times are simulated.
128 devices in a mesh: expert: 4 (over y), feat: 32 (over x, z, core).
Axes of the slice: x: 4, y: 4, z: 4, core: 2. Of those that a mesh axis runs over, the one named last changes fastest.
Arguments:
- tokens: bfloat16 [1024, 4096], P(('expert', 'feat')), may hold values from -6 to 6
- expert_ids: int32 [1024, 2], P(('expert', 'feat')), may hold values from 0 to 7, as said below
- route_weights: bfloat16 [1024, 2], P(('expert', 'feat')), may hold values from 0.099609375 to 1
- gate_proj: bfloat16 [4096, 28672], P(None, ('expert', 'feat')), may hold values from -0.09375 to 0.09375
- up_proj: bfloat16 [4096, 28672], P(None, ('expert', 'feat')), may hold values from -0.09375 to 0.09375
- down_proj: bfloat16 [28672, 4096], P(('expert', 'feat')), may hold values from -0.046875 to 0.046875
- enc_weight: float32 [4096, 32768], P(None, ('expert', 'feat')), may hold values from -0.09375 to 0.09375
- enc_bias: float32 [32768], P(('expert', 'feat')), may hold values from -3 to 3
- log_threshold: float32 [32768], P(('expert', 'feat')), may hold values from -2.3 to 0
- dec_weight: float32 [32768, 4096], P(('expert', 'feat')), may hold values from -0.046875 to 0.046875
Outputs:
- grad_encoder: float32 [4096, 32768], P(None, ('expert', 'feat'))
- grad_decoder: float32 [32768, 4096], P(('expert', 'feat'))
- grad_bias: float32 [32768], P(('expert', 'feat'))
- grad_threshold: float32 [32768], P(('expert', 'feat'))
Inputs may be any that keep to these rules, and one draw needn't show every extreme that they name: `expert_ids`: each token names two different experts of 0 to 7. Among the 8 tokens of one device, each expert below 2 is named by at most 4 tokens; in every draw one of these experts, drawn from the seed and the same for all devices, is named by exactly 4 tokens of every device.
All inputs are finite; a program needn't handle non-finite values.
Results may differ from a plain program's by a relative error of at most 0.0021.
Values may be sent and summed in bfloat16 or wider, within the bound.
A program may use at most 128 MiB of HBM per device.

v0:
```python
import jax
import jax.numpy as jnp
from jax import lax
from jax.sharding import PartitionSpec as P

sharpness = 0.1
kernel_width = 0.5
density_weight = 0.01
highest = lax.Precision.HIGHEST


def partner(block, axis, stride):
    count = lax.axis_size(axis)
    route = []
    for low in range(count):
        high = low | 1 << stride
        if high != low and high < count:
            route += [(low, high), (high, low)]
    return lax.ppermute(block, axis, route)


def pack_slots(tokens, expert_ids, route_weights, experts):
    capacity = tokens.shape[0] // 2
    window = jnp.arange(experts, dtype=jnp.int32)
    matches = expert_ids[:, :, None] == window[None, None, :]
    named = jnp.sum(matches.astype(jnp.int32), axis=1)
    weighted = jnp.sum(
        jnp.where(matches, route_weights[:, :, None], jnp.zeros((), jnp.bfloat16)), axis=1
    )
    slot_index = jnp.cumsum(named, axis=0) - named
    places = jnp.arange(capacity, dtype=jnp.int32)
    chosen = (named.T[:, None, :] == 1) & (slot_index.T[:, None, :] == places[None, :, None])
    slot_rows = jnp.einsum(
        "ect,td->ecd", chosen.astype(jnp.bfloat16), tokens, preferred_element_type=jnp.float32
    ).astype(jnp.bfloat16)
    slot_weights = jnp.sum(
        jnp.where(chosen, weighted.T[:, None, :], jnp.zeros((), jnp.bfloat16)), axis=2
    )
    return (slot_rows, slot_weights)


def contract_rows(left, right):
    return lax.dot_general(left, right, (((0,), (0,)), ((), ())), precision=highest)


def body(
    tokens,
    expert_ids,
    route_weights,
    gate_proj,
    up_proj,
    down_proj,
    enc_weight,
    enc_bias,
    log_threshold,
    dec_weight,
):
    copies = 2
    experts = lax.axis_size("expert") // copies
    slot_rows, slot_weights = pack_slots(tokens, expert_ids, route_weights, experts)
    send_rows = jnp.repeat(slot_rows, copies, axis=0)
    send_weights = jnp.repeat(slot_weights, copies, axis=0)
    came_rows, came_weights = (
        lax.all_to_all(send_rows, "expert", split_axis=0, concat_axis=0, tiled=True),
        lax.all_to_all(send_weights, "expert", split_axis=0, concat_axis=0, tiled=True),
    )
    all_rows, all_weights = (
        lax.all_gather(came_rows, "feat", axis=0, tiled=True),
        lax.all_gather(came_weights, "feat", axis=0, tiled=True),
    )
    width = tokens.shape[1]
    token_rows = all_rows.reshape(-1, width)
    row_weights = all_weights.reshape(-1).astype(jnp.float32)
    gate_act = jnp.dot(token_rows, gate_proj, preferred_element_type=jnp.float32)
    up_act = jnp.dot(token_rows, up_proj, preferred_element_type=jnp.float32)
    hidden = (jax.nn.silu(gate_act) * up_act).astype(jnp.bfloat16)
    target_part = jnp.dot(hidden, down_proj, preferred_element_type=jnp.float32)
    inputs = token_rows.astype(jnp.float32)
    preact = jnp.dot(inputs, enc_weight, precision=highest) + enc_bias
    threshold = jnp.exp(log_threshold)
    shifted = preact - threshold
    soft_gate = jax.nn.sigmoid(shifted / sharpness)
    active = preact * soft_gate
    partial_error = jnp.dot(active, dec_weight, precision=highest) - target_part
    feat_total = lax.psum(partial_error, "feat")
    recon_error = feat_total + partner(feat_total, "expert", 0)
    residual_grad = 2.0 * row_weights[:, None] * recon_error
    grad_decoder = contract_rows(active, residual_grad)
    grad_active = lax.dot_general(
        residual_grad, dec_weight, (((1,), (1,)), ((), ())), precision=highest
    )
    grad_pre = grad_active * soft_gate
    grad_encoder = contract_rows(inputs, grad_pre)
    grad_bias = jnp.sum(grad_pre, axis=0)
    kernel = jnp.maximum(0.0, 1.0 - jnp.abs(shifted) / kernel_width) / kernel_width
    slope_sum = jnp.sum(
        (grad_active * threshold + density_weight * row_weights[:, None]) * kernel, axis=0
    )
    grad_threshold = -threshold * slope_sum
    return (grad_encoder, grad_decoder, grad_bias, grad_threshold)


def solution(mesh):
    in_specs = (
        P(("expert", "feat"), None),
        P(("expert", "feat"), None),
        P(("expert", "feat"), None),
        P(None, ("expert", "feat")),
        P(None, ("expert", "feat")),
        P(("expert", "feat"), None),
        P(None, ("expert", "feat")),
        P(("expert", "feat")),
        P(("expert", "feat")),
        P(("expert", "feat"), None),
    )
    out_specs = (
        P(None, ("expert", "feat")),
        P(("expert", "feat"), None),
        P(("expert", "feat")),
        P(("expert", "feat")),
    )
    return jax.shard_map(body, mesh=mesh, in_specs=in_specs, out_specs=out_specs, check_vma=False)
```

profile of v0, /device:TPU:1, one launch (start us, length us, event | category | flops | bytes accessed | tf_op | source)
XLA Modules:
  0.0 474.6 jit_solution(3377354966974964132)
XLA Ops:
  7.2 0.8 convert_reduce_fusion
  8.1 0.2 reduce_window_sum.11
  8.2 1.0 convolution_convert_fusion
  9.3 9.7 %all_to_all.17 = bf16[4,4,4096]{2,1,0:T(4,128)(2,1)} all-to-all(bf16[4,4,4096]{2,1,0:T(4,128)(2,1)S(1)} %bitcast.20), channel_id=1, replica_groups=mesh['expert'=4,'feat'=32] {'expert'}, dimensions={0} | all-to-all | bytes 262144 | tf_op jit(solution)/shard_map/all_to_all | solution.py:64
  19.0 0.0 all-reduce.2.cloned.1.call-start
  19.1 0.7 exp.10
  19.8 48.0 %all-gather.3.cloned.1.call-done = bf16[128,4,4096]{2,1,0:T(4,128)(2,1)} async-done(((bf16[4,4,4096]{2,1,0:T(4,128)(2,1)}), bf16[128,4,4096]{2,1,0:T(4,128)(2,1)}) %all-gather.3.cloned.1.call-update) | async-done | bytes 4194320 | tf_op jit(solution)/shard_map/all_gather | solution.py:68
  67.8 6.9 %reshape.45 = bf16[512,4096]{1,0:T(8,128)(2,1)} reshape(bf16[128,4,4096]{2,1,0:T(4,128)(2,1)} %all-gather.3.cloned.1.call-done) | data formatting | bytes 8388608 | tf_op jit(solution)/shard_map/reshape | solution.py:72
  74.7 4.3 fusion.31
  79.0 5.8 %convolution_add_fusion = f32[512,256]{1,0:T(8,128)S(1)} fusion(bf16[512,4096]{1,0:T(8,128)(2,1)S(1)} %copy-done.1, f32[4096,256]{1,0:T(8,128)} %param.16, f32[256]{0:T(256)S(1)} %copy-done.7), kind=kOutput, calls=%fused_computation.6 | convolution fusion | flops 6442582016 | bytes 8913920 | tf_op jit(solution)/shard_map/dot_general | solution.py:79
  84.9 8.7 %fusion.3 = f32[512,4096]{1,0:T(8,128)} fusion(bf16[224,4096]{1,0:T(8,128)(2,1)S(1)} %copy-done, bf16[512,4096]{1,0:T(8,128)(2,1)} %reshape.45, bf16[4096,224]{0,1:T(8,128)(2,1)} %param.14, f32[512,224]{0,1:T(8,128)S(1)} %fusion.31), kind=kOutput, calls=%fused_computation.8 | convolution fusion | flops 1879736320 | bytes 16711680 | tf_op jit(solution)/shard_map/dot_general | solution.py:77
  93.6 13.0 %convolution_subtract_fusion = f32[512,4096]{1,0:T(8,128)} fusion(f32[512,4096]{1,0:T(8,128)} %fusion.3, f32[256,4096]{1,0:T(8,128)} %param.19, f32[512,256]{1,0:T(8,128)S(1)} %convolution_add_fusion, f32[256]{0:T(256)S(1)} %exp.10), kind=kOutput, calls=%fused_computation.1 | convolution fusion | flops 6445334528 | bytes 21496832 | tf_op jit(solution)/shard_map/dot_general | solution.py:84
  106.6 119.7 %all-reduce.2.cloned.1.call-done = f32[512,4096]{1,0:T(8,128)} async-done(((f32[512,4096]{1,0:T(8,128)}), f32[512,4096]{1,0:T(8,128)}) %all-reduce.2.cloned.1.call-update) | async-done | bytes 8388624 | tf_op jit(solution)/shard_map/psum | solution.py:85
  226.4 1.2 collective-permute-start
  227.6 0.1 fusion.18
  227.7 181.8 %all_to_all.18 = bf16[4,1,4]{2,1,0:T(2,128)(2,1)S(1)} all-to-all(bf16[4,1,4]{2,1,0:T(2,128)(2,1)S(1)} %copy.21), channel_id=1, replica_groups=mesh['expert'=4,'feat'=32] {'expert'}, dimensions={0} | all-to-all | bytes 64 | tf_op jit(solution)/shard_map/all_to_all | solution.py:65
  409.5 26.1 %all-gather = bf16[128,1,4]{2,1,0:T(2,128)(2,1)S(1)} all-gather(bf16[4,1,4]{2,1,0:T(2,128)(2,1)S(1)} %all_to_all.18), channel_id=2, replica_groups=mesh['expert'=4,'feat'=32] {'feat'}, dimensions={0}, use_global_device_ids=true | all-gather | bytes 1056 | tf_op jit(solution)/shard_map/all_gather | solution.py:69
  435.6 0.4 multiply_reduce_fusion.1
  436.0 0.1 mul.73
  436.1 0.1 mul.63
  436.2 13.2 %multiply_reduce_fusion = (f32[256]{0:T(256)S(1)}, f32[256]{0:T(256)}, f32[512,256]{1,0:T(8,128)S(1)}) fusion(f32[512,256]{1,0:T(8,128)S(1)} %convolution_add_fusion, f32[512]{0:T(512)S(1)} %mul.73, f32[256]{0:T(256)S(1)} %exp.10, f32[256,4096]{1,0:T(8,128)} %param.19, f32[512,4096]{1,0:T(8,128)} %all-reduce.2.cloned.1.call-done, ...), kind=kOutput, calls=%fused_computation.9 | convolution fusion | flops 6448741888 | bytes 22027264 | tf_op jit(solution)/shard_map/dot_general | solution.py:89
  449.4 6.3 %fusion.29 = f32[4096,256]{1,0:T(8,128)} fusion(bf16[512,4096]{1,0:T(8,128)(2,1)S(1)} %copy-done.2, f32[512,256]{1,0:T(8,128)S(1)} %get-tuple-element.8, f32[512,256]{1,0:T(8,128)S(1)} %convolution_add_fusion, f32[256]{0:T(256)S(1)} %exp.10), kind=kOutput, calls=%fused_computation.41 | convolution fusion | flops 6443237376 | bytes 9438208 | tf_op jit(solution)/shard_map/dot_general | solution.py:43
  455.7 0.6 negate_multiply_fusion
  456.3 11.5 %fusion = f32[256,4096]{1,0:T(8,128)} fusion(f32[512,4096]{1,0:T(8,128)S(1)} %copy-done.3, f32[512,4096]{1,0:T(8,128)} %collective-permute-done, f32[512]{0:T(512)S(1)} %mul.63, f32[512,256]{1,0:T(8,128)S(1)} %convolution_add_fusion, f32[256]{0:T(256)S(1)} %exp.10), kind=kOutput, calls=%fused_computation.4 | convolution fusion | flops 6447431680 | bytes 21498880 | tf_op jit(solution)/shard_map/dot_general | solution.py:43
  (26 shorter events, 0.2 us)
Async XLA Ops:
  7.2 77.7 %copy-start = (bf16[224,4096]{1,0:T(8,128)(2,1)S(1)}, bf16[224,4096]{1,0:T(8,128)(2,1)}, u32[]{:S(2)}) copy-start(bf16[224,4096]{1,0:T(8,128)(2,1)} %param.15) | copy-start | bytes 5505028
  7.2 60.6 %all-gather.3.cloned.1.call-start = ((), (), s32[]{:S(2)}) async-start(), calls=%async_computation.2 | async-start | bytes 4325376 | tf_op jit(solution)/shard_map/all_gather | solution.py:68
  19.0 207.3 %all-reduce.2.cloned.1.call-start = ((), (), s32[]{:S(2)}) async-start(), calls=%async_computation.3 | async-start | bytes 16777216 | tf_op jit(solution)/shard_map/psum | solution.py:85
  74.7 4.4 copy-start.1
  74.7 4.4 copy-start.7
  106.6 121.0 %copy-start.5 = (s32[8,2]{0,1:T(2,128)S(1)}, s32[8,2]{0,1:T(2,128)}, u32[]{:S(2)}) copy-start(s32[8,2]{0,1:T(2,128)} %param.11) | copy-start | bytes 196
  106.6 121.0 %copy-start.6 = (bf16[8,2]{0,1:T(2,128)(2,1)S(1)}, bf16[8,2]{0,1:T(2,128)(2,1)}, u32[]{:S(2)}) copy-start(bf16[8,2]{0,1:T(2,128)(2,1)} %param.12) | copy-start | bytes 100
  226.4 209.8 %collective-permute-start = (f32[512,4096]{1,0:T(8,128)}, f32[512,4096]{1,0:T(8,128)}, u32[]{:S(2)}, u32[]{:S(2)}) collective-permute-start(f32[512,4096]{1,0:T(8,128)} %all-reduce.2.cloned.1.call-done), channel_id=1, source_target_pairs={{0,32},{32,0},{64,96},{96,64},{1,33},{33,1},{65,97},{97,65},{2,34}... | collective-permute-start | bytes 25165832 | tf_op jit(solution)/shard_map/ppermute | solution.py:19
  436.2 13.2 %copy-start.2 = (bf16[512,4096]{1,0:T(8,128)(2,1)S(1)}, bf16[512,4096]{1,0:T(8,128)(2,1)}, u32[]{:S(2)}) copy-start(bf16[512,4096]{1,0:T(8,128)(2,1)} %reshape.45) | copy-start | bytes 12582916
  449.4 6.3 %copy-start.4 = (f32[256]{0:T(256)S(1)}, f32[256]{0:T(256)}, u32[]{:S(2)}) copy-start(f32[256]{0:T(256)} %param.18) | copy-start | bytes 3076
  449.4 6.9 %copy-start.3 = (f32[512,4096]{1,0:T(8,128)S(1)}, f32[512,4096]{1,0:T(8,128)}, u32[]{:S(2)}) copy-start(f32[512,4096]{1,0:T(8,128)} %all-reduce.2.cloned.1.call-done) | copy-start | bytes 25165828
Sparse Core Ops, SparseCore 0:
  19.2 48.5 all-gather.2
  106.8 119.5 all-reduce.1
where the time goes:
time: 475 us
  blocking collectives  218 us (46%)
  waiting for transfers between devices  168 us (35%)
  matrix products  63.9 us (13%)
  between operations  14.1 us (3%)
  local copies, waits for them, and re-layouts  7.86 us (2%)
    all_to_all x1, blocking collectives, body(): lax.all_to_all(send_weights, 'expert', split_axis=0, concat_axis=0, tiled...  182 us
    psum x1, waiting for transfers between devices, body(): feat_total = lax.psum(partial_error, 'feat')  120 us
    all_gather x1, waiting for transfers between devices, body(): lax.all_gather(came_rows, 'feat', axis=0, tiled=True)  48 us
    all_gather x1, blocking collectives, body(): lax.all_gather(came_weights, 'feat', axis=0, tiled=True)  26.1 us
    dot_general x2, matrix products, contract_rows(): lax.dot_general(left, right, (((0,), (0,)), ((), ())), precision=highest)  17.8 us
    dot_general x1, matrix products, body(): lax.dot_general(residual_grad, dec_weight, (((1,), (1,)), ((), ())), prec...  13.2 us
    dot_general x1, matrix products, body(): partial_error = jnp.dot(active, dec_weight, precision=highest) - target_part  13 us
    all_to_all x1, blocking collectives, body(): lax.all_to_all(send_rows, 'expert', split_axis=0, concat_axis=0, tiled=True)  9.75 us
  transfers between devices with their start and end apart: 3, of which 2 were waited for; matrix products, arithmetic and copies ran while one was open for 0% of the time, Pallas kernels for 0%

commit v1 on v0

--- a/solution.py
+++ b/solution.py
@@ -6,7 +6,6 @@
 sharpness = 0.1
 kernel_width = 0.5
 density_weight = 0.01
-highest = lax.Precision.HIGHEST
 
 
 def partner(block, axis, stride):
@@ -27,7 +26,9 @@
     weighted = jnp.sum(
         jnp.where(matches, route_weights[:, :, None], jnp.zeros((), jnp.bfloat16)), axis=1
     )
-    slot_index = jnp.cumsum(named, axis=0) - named
+    rows = jnp.arange(tokens.shape[0], dtype=jnp.int32)
+    earlier = rows[None, :, None] < rows[:, None, None]
+    slot_index = jnp.sum(jnp.where(earlier, named[None, :, :], 0), axis=1)
     places = jnp.arange(capacity, dtype=jnp.int32)
     chosen = (named.T[:, None, :] == 1) & (slot_index.T[:, None, :] == places[None, :, None])
     slot_rows = jnp.einsum(
@@ -39,8 +40,13 @@
     return (slot_rows, slot_weights)
 
 
-def contract_rows(left, right):
-    return lax.dot_general(left, right, (((0,), (0,)), ((), ())), precision=highest)
+def split(value):
+    high = lax.reduce_precision(value, 8, 7)
+    return high.astype(jnp.bfloat16), (value - high).astype(jnp.bfloat16)
+
+
+def product(left, right, dims):
+    return lax.dot_general(left, right, (dims, ((), ())), preferred_element_type=jnp.float32)
 
 
 def body(
@@ -75,22 +81,30 @@
     up_act = jnp.dot(token_rows, up_proj, preferred_element_type=jnp.float32)
     hidden = (jax.nn.silu(gate_act) * up_act).astype(jnp.bfloat16)
     target_part = jnp.dot(hidden, down_proj, preferred_element_type=jnp.float32)
-    inputs = token_rows.astype(jnp.float32)
-    preact = jnp.dot(inputs, enc_weight, precision=highest) + enc_bias
+    rows = ((1,), (0,))
+    down = ((0,), (0,))
+    enc_high, enc_low = split(enc_weight)
+    dec_high, dec_low = split(dec_weight)
+    preact = product(token_rows, enc_high, rows) + product(token_rows, enc_low, rows) + enc_bias
     threshold = jnp.exp(log_threshold)
     shifted = preact - threshold
     soft_gate = jax.nn.sigmoid(shifted / sharpness)
     active = preact * soft_gate
-    partial_error = jnp.dot(active, dec_weight, precision=highest) - target_part
-    feat_total = lax.psum(partial_error, "feat")
+    act_high, act_low = split(active)
+    recon = product(act_high, dec_high, rows) + product(act_high, dec_low, rows)
+    partial_error = recon + product(act_low, dec_high, rows) - target_part
+    feat_total = lax.psum_scatter(partial_error, "feat", scatter_dimension=0, tiled=True)
     recon_error = feat_total + partner(feat_total, "expert", 0)
-    residual_grad = 2.0 * row_weights[:, None] * recon_error
-    grad_decoder = contract_rows(active, residual_grad)
-    grad_active = lax.dot_general(
-        residual_grad, dec_weight, (((1,), (1,)), ((), ())), precision=highest
-    )
+    own_rows = feat_total.shape[0]
+    own_weights = lax.dynamic_slice_in_dim(row_weights, lax.axis_index("feat") * own_rows, own_rows)
+    own_grad = (2.0 * own_weights[:, None] * recon_error).astype(jnp.bfloat16)
+    residual_grad = lax.all_gather(own_grad, "feat", axis=0, tiled=True)
+    grad_decoder = product(act_high, residual_grad, down) + product(act_low, residual_grad, down)
+    across = ((1,), (1,))
+    grad_active = product(residual_grad, dec_high, across) + product(residual_grad, dec_low, across)
     grad_pre = grad_active * soft_gate
-    grad_encoder = contract_rows(inputs, grad_pre)
+    pre_high, pre_low = split(grad_pre)
+    grad_encoder = product(token_rows, pre_high, down) + product(token_rows, pre_low, down)
     grad_bias = jnp.sum(grad_pre, axis=0)
     kernel = jnp.maximum(0.0, 1.0 - jnp.abs(shifted) / kernel_width) / kernel_width
     slope_sum = jnp.sum(

time: 475 us -> 314 us (0.66)
  blocking collectives: 218 us -> 37.3 us
  waiting for transfers between devices: 168 us -> 185 us
  matrix products: 63.9 us -> 57.1 us
    all_to_all x1 -> x0, blocking collectives: 182 us -> none  [body(): lax.all_to_all(send_weights, 'expert', split_axis=0, concat_axis=0, tiled...]
    psum x1 -> x0, waiting for transfers between devices: 120 us -> none  [body(): feat_total = lax.psum(partial_error, 'feat')]
    reduce_scatter x0 -> x1, waiting for transfers between devices: none -> 89.5 us  [body(): lax.psum_scatter(partial_error, 'feat', scatter_dimension=0, tiled=True)]
    all_gather x0 -> x1, waiting for transfers between devices: none -> 43.2 us  [body(): residual_grad = lax.all_gather(own_grad, 'feat', axis=0, tiled=True)]
    dot_general x5 -> x11, matrix products: 49.8 us -> 45.9 us  [product(): lax.dot_general(left, right, (dims, ((), ())), preferred_element_type=jnp...]
  transfers between devices with their start and end apart: 3 -> 5, of which waited for: 2 -> 4; matrix products, arithmetic and copies ran while one was open for 0% -> 1% of each run, Pallas kernels for 0% -> 0%
where the time goes in v1:
time: 314 us
  waiting for transfers between devices  185 us (59%)
  matrix products  57.1 us (18%)
  blocking collectives  37.3 us (12%)
  between operations  13.9 us (4%)
  local copies, waits for them, and re-layouts  11.9 us (4%)
  starting transfers between devices  4.98 us (2%)
  other arithmetic  3.61 us (1%)
    reduce_scatter x1, waiting for transfers between devices, body(): lax.psum_scatter(partial_error, 'feat', scatter_dimension=0, tiled=True)  89.5 us
    all_gather x1, waiting for transfers between devices, body(): lax.all_gather(came_rows, 'feat', axis=0, tiled=True)  48 us
    dot_general x11, matrix products, product(): lax.dot_general(left, right, (dims, ((), ())), preferred_element_type=jnp...  45.9 us
    all_gather x1, waiting for transfers between devices, body(): residual_grad = lax.all_gather(own_grad, 'feat', axis=0, tiled=True)  43.2 us
    all_gather x1, blocking collectives, body(): lax.all_gather(came_weights, 'feat', axis=0, tiled=True)  27.5 us
    all_to_all x1, blocking collectives, body(): lax.all_to_all(send_rows, 'expert', split_axis=0, concat_axis=0, tiled=True)  9.75 us
    dot_general x1, matrix products, body(): target_part = jnp.dot(hidden, down_proj, preferred_element_type=jnp.float32)  8.72 us
    reshape x1, local copies, waits for them, and re-layouts, body(): token_rows = all_rows.reshape(-1, width)  6.87 us
  transfers between devices with their start and end apart: 5, of which 4 were waited for; matrix products, arithmetic and copies ran while one was open for 1% of the time, Pallas kernels for 0%

profile of v1, /device:TPU:1, one launch (start us, length us, event | category | flops | bytes accessed | tf_op | source)
XLA Modules:
  0.0 313.5 jit_solution(17543353753348144969)
XLA Ops:
  9.3 9.7 %all_to_all.17 = bf16[4,4,4096]{2,1,0:T(4,128)(2,1)} all-to-all(bf16[4,4,4096]{2,1,0:T(4,128)(2,1)S(1)} %bitcast.22), channel_id=1, replica_groups=mesh['expert'=4,'feat'=32] {'expert'}, dimensions={0} | all-to-all | bytes 262144 | tf_op jit(solution)/shard_map/all_to_all | solution.py:70
  19.8 48.0 %all-gather.4.cloned.1.call-done = bf16[128,4,4096]{2,1,0:T(4,128)(2,1)} async-done(((bf16[4,4,4096]{2,1,0:T(4,128)(2,1)}), bf16[128,4,4096]{2,1,0:T(4,128)(2,1)}) %all-gather.4.cloned.1.call-update) | async-done | bytes 4194320 | tf_op jit(solution)/shard_map/all_gather | solution.py:74
  67.8 6.9 %reshape.55 = bf16[512,4096]{1,0:T(8,128)(2,1)} reshape(bf16[128,4,4096]{2,1,0:T(4,128)(2,1)} %all-gather.4.cloned.1.call-done) | data formatting | bytes 8388608 | tf_op jit(solution)/shard_map/reshape | solution.py:78
  74.6 4.9 %fusion.2 = f32[512,256]{1,0:T(8,128)S(1)} fusion(bf16[512,4096]{1,0:T(8,128)(2,1)} %reshape.55, f32[4096,256]{1,0:T(8,128)} %param.16), kind=kOutput, calls=%fused_computation.10 | convolution fusion | flops 1076887552 | bytes 8912896 | tf_op jit(solution)/shard_map/dot_general | solution.py:49
  79.5 1.0 copy-done.7
  80.6 1.3 fusion.6
  82.8 4.6 %fusion.11 = f32[512,4096]{1,0:T(8,128)} fusion(f32[256,4096]{1,0:T(8,128)S(1)} %copy-done.5, f32[512,256]{1,0:T(8,128)S(1)} %fusion.6, f32[256]{0:T(256)S(1)} %exp.10), kind=kOutput, calls=%fused_computation.23 | convolution fusion | flops 1077936128 | bytes 13108224 | tf_op jit(solution)/shard_map/dot_general | solution.py:49
  87.3 4.5 %fusion.38 = f32[512,4096]{1,0:T(8,128)} fusion(f32[256,4096]{1,0:T(8,128)S(1)} %copy-done.5, f32[512,256]{1,0:T(8,128)S(1)} %fusion.6, f32[256]{0:T(256)S(1)} %exp.10), kind=kOutput, calls=%fused_computation.58 | convolution fusion | flops 1076887552 | bytes 13108224 | tf_op jit(solution)/shard_map/dot_general | solution.py:49
  91.9 1.4 fusion.46
  93.3 8.7 %fusion.8 = f32[512,4096]{1,0:T(8,128)} fusion(bf16[224,4096]{1,0:T(8,128)(2,1)S(1)} %copy-done, bf16[512,4096]{1,0:T(8,128)(2,1)} %reshape.55, bf16[4096,224]{0,1:T(8,128)(2,1)} %param.14, f32[512,224]{0,1:T(8,128)S(1)} %fusion.46), kind=kOutput, calls=%fused_computation.17 | convolution fusion | flops 1879736320 | bytes 16711680 | tf_op jit(solution)/shard_map/dot_general | solution.py:83
  102.0 14.3 %add_subtract_fusion = f32[512,4096]{1,0:T(8,128)} fusion(f32[512,4096]{1,0:T(8,128)} %fusion.8, f32[512,4096]{1,0:T(8,128)} %fusion.38, f32[512,4096]{1,0:T(8,128)} %fusion.11, f32[256,4096]{1,0:T(8,128)} %param.19, f32[512,256]{1,0:T(8,128)S(1)} %fusion.6, f32[256]{0:T(256)S(1)} %exp.10), kind=kOutput, calls=%fused_computation | convolution fusion | flops 1083310080 | bytes 38274048 | tf_op jit(solution)/shard_map/dot_general | solution.py:49
  117.0 89.5 %reduce-scatter.2.cloned.1.call-done = f32[16,4096]{1,0:T(8,128)} async-done(((f32[512,4096]{1,0:T(8,128)}), f32[16,4096]{1,0:T(8,128)}) %reduce-scatter.2.cloned.1.call-update) | async-done | bytes 262160 | tf_op jit(solution)/shard_map/reduce_scatter | solution.py:96
  206.5 1.2 collective-permute-start
  208.4 3.7 %all-to-all-start.1 = ((bf16[4,1,4]{2,1,0:T(2,128)(2,1)}), bf16[4,1,4]{2,1,0:T(2,128)(2,1)S(1)}, u32[]{:S(2)}, u32[]{:S(2)}) async-start(bf16[4,1,4]{2,1,0:T(2,128)(2,1)} %copy.24), calls=%async_computation.1 | async-start | bytes 4096 | tf_op jit(solution)/shard_map/all_to_all | solution.py:71
  212.1 4.1 %all-to-all-done.1 = bf16[4,1,4]{2,1,0:T(2,128)(2,1)S(1)} async-done(((bf16[4,1,4]{2,1,0:T(2,128)(2,1)}), bf16[4,1,4]{2,1,0:T(2,128)(2,1)S(1)}, u32[]{:S(2)}, u32[]{:S(2)}) %all-to-all-start.1) | async-done | bytes 64 | tf_op jit(solution)/shard_map/all_to_all | solution.py:71
  216.2 27.5 %all-gather = bf16[128,1,4]{2,1,0:T(2,128)(2,1)S(1)} all-gather(bf16[4,1,4]{2,1,0:T(2,128)(2,1)S(1)} %all-to-all-done.1), channel_id=2, replica_groups=mesh['expert'=4,'feat'=32] {'feat'}, dimensions={0}, use_global_device_ids=true | all-gather | bytes 1056 | tf_op jit(solution)/shard_map/all_gather | solution.py:75
  244.1 1.7 multiply_convert_fusion
  245.8 43.2 %all-gather.6.cloned.1.call-done = bf16[512,4096]{1,0:T(8,128)(2,1)} async-done(((bf16[16,4096]{1,0:T(8,128)(2,1)}), bf16[512,4096]{1,0:T(8,128)(2,1)}) %all-gather.6.cloned.1.call-update) | async-done | bytes 4194320 | tf_op jit(solution)/shard_map/all_gather | solution.py:101
  289.0 4.9 %fusion.9 = f32[512,256]{1,0:T(8,128)S(1)} fusion(bf16[512,4096]{1,0:T(8,128)(2,1)} %all-gather.6.cloned.1.call-done, f32[256,4096]{1,0:T(8,128)} %param.19), kind=kOutput, calls=%fused_computation.22 | convolution fusion | flops 1076887552 | bytes 8912896 | tf_op jit(solution)/shard_map/dot_general | solution.py:49
  294.9 2.0 fusion.44
  297.5 1.3 fusion.23
  298.8 3.3 %convolution_add_fusion.1 = f32[4096,256]{1,0:T(8,128)} fusion(f32[4096,256]{1,0:T(8,128)S(1)} %fusion.23, bf16[512,4096]{1,0:T(8,128)(2,1)S(1)} %copy-done.3, f32[512,256]{1,0:T(8,128)S(1)} %get-tuple-element.5), kind=kOutput, calls=%fused_computation.6 | convolution fusion | flops 1075183616 | bytes 13107200 | tf_op jit(solution)/shard_map/dot_general | solution.py:49
  302.1 1.4 fusion.25
  303.5 3.5 %convolution_add_fusion = f32[256,4096]{1,0:T(8,128)} fusion(f32[256,4096]{1,0:T(8,128)S(1)} %fusion.25, bf16[512,4096]{1,0:T(8,128)(2,1)S(1)} %copy-done.4, f32[512,256]{1,0:T(8,128)S(1)} %fusion.6, f32[256]{0:T(256)S(1)} %exp.10), kind=kOutput, calls=%fused_computation.5 | convolution fusion | flops 1075838976 | bytes 13108224 | tf_op jit(solution)/shard_map/dot_general | solution.py:49
  (48 shorter events, 7.1 us)
Async XLA Ops:
  7.2 86.1 %copy-start = (bf16[224,4096]{1,0:T(8,128)(2,1)S(1)}, bf16[224,4096]{1,0:T(8,128)(2,1)}, u32[]{:S(2)}) copy-start(bf16[224,4096]{1,0:T(8,128)(2,1)} %param.15) | copy-start | bytes 5505028
  7.2 60.6 %all-gather.4.cloned.1.call-start = ((), (), s32[]{:S(2)}) async-start(), calls=%async_computation.3 | async-start | bytes 4325376 | tf_op jit(solution)/shard_map/all_gather | solution.py:74
  19.0 187.5 %reduce-scatter.2.cloned.1.call-start = ((), (), s32[]{:S(2)}) async-start(), calls=%async_computation.4 | async-start | bytes 8650752 | tf_op jit(solution)/shard_map/reduce_scatter | solution.py:96
  74.6 4.9 %copy-start.2 = (bf16[512,4096]{1,0:T(8,128)(2,1)S(1)}, bf16[512,4096]{1,0:T(8,128)(2,1)}, u32[]{:S(2)}) copy-start(bf16[512,4096]{1,0:T(8,128)(2,1)} %reshape.55) | copy-start | bytes 12582916
  74.6 5.9 %copy-start.7 = (f32[4096,256]{1,0:T(8,128)S(1)}, f32[4096,256]{1,0:T(8,128)}, u32[]{:S(2)}) copy-start(f32[4096,256]{1,0:T(8,128)} %param.16) | copy-start | bytes 12582916
  74.6 5.9 %copy-start.8 = (f32[256]{0:T(256)S(1)}, f32[256]{0:T(256)}, u32[]{:S(2)}) copy-start(f32[256]{0:T(256)} %param.17) | copy-start | bytes 3076
  80.6 2.2 copy-start.5
  87.3 4.5 %copy-start.12 = (bf16[4096,224]{0,1:T(8,128)(2,1)S(1)}, bf16[4096,224]{0,1:T(8,128)(2,1)}, u32[]{:S(2)}) copy-start(bf16[4096,224]{0,1:T(8,128)(2,1)} %param.13) | copy-start | bytes 5505028
  116.3 0.7 copy-start.10
  116.3 0.7 copy-start.11
  206.5 37.6 %collective-permute-start = (f32[16,4096]{1,0:T(8,128)}, f32[16,4096]{1,0:T(8,128)S(1)}, u32[]{:S(2)}, u32[]{:S(2)}) collective-permute-start(f32[16,4096]{1,0:T(8,128)} %reduce-scatter.2.cloned.1.call-done), channel_id=1, source_target_pairs={{0,32},{32,0},{64,96},{96,64},{1,33},{33,1},{65,97},{97,65},{2,34}... | collective-permute-start | bytes 786440 | tf_op jit(solution)/shard_map/ppermute | solution.py:18
  208.4 7.8 %all-to-all-start.1 = ((bf16[4,1,4]{2,1,0:T(2,128)(2,1)}), bf16[4,1,4]{2,1,0:T(2,128)(2,1)S(1)}, u32[]{:S(2)}, u32[]{:S(2)}) async-start(bf16[4,1,4]{2,1,0:T(2,128)(2,1)} %copy.24), calls=%async_computation.1 | async-start | bytes 4096 | tf_op jit(solution)/shard_map/all_to_all | solution.py:71
  212.1 76.9 %all-gather.6.cloned.1.call-start = ((), (), s32[]{:S(2)}) async-start(), calls=%async_computation.5 | async-start | bytes 4325376 | tf_op jit(solution)/shard_map/all_gather | solution.py:101
  289.0 4.9 %copy-start.4 = (bf16[512,4096]{1,0:T(8,128)(2,1)S(1)}, bf16[512,4096]{1,0:T(8,128)(2,1)}, u32[]{:S(2)}) copy-start(bf16[512,4096]{1,0:T(8,128)(2,1)} %all-gather.6.cloned.1.call-done) | copy-start | bytes 12582916
  289.0 5.9 %copy-start.6 = (f32[256,4096]{1,0:T(8,128)S(1)}, f32[256,4096]{1,0:T(8,128)}, u32[]{:S(2)}) copy-start(f32[256,4096]{1,0:T(8,128)} %param.19) | copy-start | bytes 12582916
  294.9 2.0 copy-start.9
  294.9 2.6 copy-start.3
  302.1 4.9 %copy-start.1 = (bf16[224,4096]{1,0:T(8,128)(2,1)S(1)}, bf16[224,4096]{1,0:T(8,128)(2,1)}, u32[]{:S(2)}) copy-start(bf16[224,4096]{1,0:T(8,128)(2,1)} %param.15) | copy-start | bytes 5505028
Sparse Core Ops, SparseCore 0:
  19.1 48.5 all-gather.3
  116.5 89.9 reduce-scatter.1
  245.9 43.0 all-gather.5

commit v2 on v0

v2 whole, which is shorter than its diff:
```python
import functools

import jax
import jax.numpy as jnp
from jax import lax
from jax.experimental import pallas as pl
from jax.experimental.pallas import tpu as pltpu
from jax.sharding import PartitionSpec as P

MESH = pl.DeviceIdType.MESH
f32 = jnp.float32
bf16 = jnp.bfloat16

sharpness = 0.1
kernel_width = 0.5
density_weight = 0.01

CHUNKS = 2
LANES = 128
UNIT = 16
BLOCK = 4 * UNIT
HALF = 4 * BLOCK
ROWS = 2 * HALF


def dot(left, right):
    return jnp.dot(left, right, preferred_element_type=f32)


def dot_nt(left, right):
    return lax.dot_general(left, right, (((1,), (1,)), ((), ())), preferred_element_type=f32)


def dot_tn(left, right):
    return lax.dot_general(left, right, (((0,), (0,)), ((), ())), preferred_element_type=f32)


def split(value):
    high = value.astype(bf16)
    return high, (value - high.astype(f32)).astype(bf16)


def encode(value, out, rows):
    width = value.shape[1]
    largest = jnp.max(jnp.abs(value), axis=1, keepdims=True)
    power = jnp.ceil(jnp.log2(jnp.maximum(largest, 1e-30)))
    out[rows, 0:width] = jnp.round(value * jnp.exp2(14.0 - power)).astype(jnp.int32).astype(jnp.int16)
    lanes = jnp.broadcast_to(power.astype(jnp.int32), (value.shape[0], LANES))
    out[rows, width : width + LANES] = lanes.astype(jnp.int16)


def decode(ref, rows):
    width = ref.shape[1] - LANES
    power = ref[rows, width : width + LANES].astype(jnp.int32).astype(f32)[:, 0:1]
    return ref[rows, 0:width].astype(jnp.int32).astype(f32) * jnp.exp2(power - 14.0)


def each(count, step):
    lax.fori_loop(0, count, lambda i, carry: (step(i), carry)[1], 0)


def al(start, size):
    return pl.ds(pl.multiple_of(start, 16), size)


def forward_kernel(
    tokens,
    ids,
    weights,
    bias,
    log_threshold,
    gate_hbm,
    up_hbm,
    down_hbm,
    enc_hbm,
    dec_hbm,
    rows_out,
    grad_out,
    act_high_out,
    act_low_out,
    pre_high_out,
    pre_low_out,
    bias_out,
    threshold_out,
    enc_stage,
    dec_stage,
    gate_w,
    up_w,
    enc_w,
    dec_w,
    pack32,
    pack,
    ybuf,
    unit32,
    trows,
    rgrad,
    acc_gate,
    acc_up,
    acc_pre,
    left,
    gate_s,
    shift_s,
    acc_grad,
    psib,
    pown,
    sib_out,
    sib_in,
    b1_out,
    b1_in,
    b2_out,
    b2_in,
    a_out,
    a_in,
    y_out,
    y_in,
    send_sem,
    recv_sem,
    ysend_sem,
    yrecv_sem,
    local_sem,
):
    width = tokens.shape[1]
    cols = width // CHUNKS
    hidden_width = gate_w.shape[1]
    features = enc_w.shape[1] // 2
    piece = width // 4

    y = lax.axis_index("expert")
    feat = lax.axis_index("feat")
    core = lax.rem(feat, 2)
    z = lax.rem(feat // 2, 4)
    x = feat // 8
    a = x + core * (z - x)
    b = z + core * (x - z)

    def a_peer(k):
        ax = lax.rem(x + (1 - core) * k, 4)
        az = lax.rem(z + core * k, 4)
        return (y, (ax * 4 + az) * 2 + core)

    def b_peer(k):
        bx = lax.rem(x + core * k, 4)
        bz = lax.rem(z + (1 - core) * k, 4)
        return (y, (bx * 4 + bz) * 2 + core)

    def y_peer(k):
        return (lax.rem(y + k, 4), feat)

    sibling = (y, feat + 1 - 2 * core)
    partner = (y + 1 - 2 * lax.rem(y, 2), feat)

    loads = [
        pltpu.make_async_copy(src, dst, local_sem.at[i])
        for i, (src, dst) in enumerate(
            [
                (enc_hbm, enc_stage),
                (dec_hbm, dec_stage),
                (gate_hbm, gate_w),
                (up_hbm, up_w),
                (down_hbm, dec_w.at[pl.ds(3 * features, hidden_width)]),
            ]
        )
    ]
    for load in loads:
        load.start()

    barrier = pltpu.get_barrier_semaphore()
    peers = [a_peer(k) for k in (1, 2, 3)] + [b_peer(k) for k in (1, 3)] + [y_peer(k) for k in (1, 2, 3)] + [sibling]
    for peer in peers:
        pl.semaphore_signal(barrier, inc=1, device_id=peer, device_id_type=MESH)

    row_id = lax.broadcasted_iota(jnp.int32, (8, 1), 0)
    values = tokens[...].astype(f32)
    route = weights[...].astype(f32)
    for expert in range(2):
        match = ids[...] == expert
        named = jnp.sum(jnp.where(match, 1.0, 0.0), axis=1, keepdims=True)
        weight = jnp.sum(jnp.where(match, route, 0.0), axis=1, keepdims=True)
        slot = jnp.zeros((8, 1), f32)
        for t in range(7):
            slot += jnp.where(row_id > t, named[t : t + 1, :], 0.0)
        pack32[...] = jnp.zeros_like(pack32)
        for c in range(4):
            chosen = jnp.where(jnp.logical_and(named > 0.5, jnp.abs(slot - c) < 0.5), 1.0, 0.0)
            row = jnp.sum(chosen * values, axis=0, keepdims=True)
            for q in range(4):
                pack32[c * 4 + q : c * 4 + q + 1, 0:piece] = row[:, q * piece : (q + 1) * piece]
            total = jnp.sum(chosen * weight, axis=0, keepdims=True)
            pack32[c * 4 : c * 4 + 1, piece : piece + LANES] = jnp.broadcast_to(total, (1, LANES))
        pack[expert] = pack32[...].astype(bf16)

    pl.semaphore_wait(barrier, len(peers))

    sends = []

    def remote(src, dst, peer, chunk, number):
        copy = pltpu.make_async_remote_copy(
            src_ref=src,
            dst_ref=dst,
            send_sem=send_sem.at[chunk, number],
            recv_sem=recv_sem.at[chunk, number],
            device_id=peer,
            device_id_type=MESH,
        )
        copy.start()
        sends.append(copy)
        return copy

    y_copies = []
    for k in (1, 2, 3):
        target = y_peer(k)
        copy = pltpu.make_async_remote_copy(
            src_ref=pack.at[target[0] // 2],
            dst_ref=ybuf.at[y],
            send_sem=ysend_sem.at[k - 1],
            recv_sem=yrecv_sem.at[k - 1],
            device_id=target,
            device_id_type=MESH,
        )
        copy.start()
        sends.append(copy)
        y_copies.append(copy)
    ybuf[y] = pack[y // 2]

    loads[0].wait()

    def split_enc(i):
        r = pl.ds(pl.multiple_of(i * 128, 128), 128)
        enc_w[r, 0:features], enc_w[r, features : 2 * features] = split(enc_stage[r, :])

    each(width // 128, split_enc)

    for copy in y_copies:
        copy.wait_recv()
    for s in range(4):
        came = ybuf[s].astype(f32)
        for c in range(4):
            for q in range(4):
                at = LANES + q * piece
                unit32[s * 4 + c : s * 4 + c + 1, at : at + piece] = came[c * 4 + q : c * 4 + q + 1, 0:piece]
            unit32[s * 4 + c : s * 4 + c + 1, 0:LANES] = came[c * 4 : c * 4 + 1, piece : piece + LANES]
    own_unit = (core * 16 + b * 4 + a) * UNIT
    trows[al(own_unit, UNIT), :] = unit32[...].astype(bf16)

    def block_rows(k):
        return core * HALF + lax.rem(b + k, 4) * BLOCK

    def gather_stages(ref, lane_ranges, base):
        copies = {}

        def go(k, start, size, peer, number):
            part = ref.at[al(start, size), lane_ranges[k]]
            copies[k, number] = remote(part, part, peer, k, base + number)

        def along_a(k):
            for i in (1, 2, 3):
                go(k, own_unit, UNIT, a_peer(i), i - 1)

        def along_b(k):
            for i in (1, 2, 3):
                copies[k, i - 1].wait_recv()
            go(k, block_rows(0), BLOCK, b_peer(1), 3)
            go(k, block_rows(0), BLOCK, b_peer(3), 4)
            go(k, block_rows(0), BLOCK, sibling, 7)

        def onward(k):
            copies[k, 3].wait_recv()
            go(k, block_rows(3), BLOCK // 2, b_peer(1), 5)
            go(k, block_rows(3), BLOCK, sibling, 8)
            copies[k, 4].wait_recv()
            go(k, block_rows(1) + BLOCK // 2, BLOCK // 2, b_peer(3), 6)
            go(k, block_rows(1), BLOCK, sibling, 9)

        def last(k):
            copies[k, 5].wait_recv()
            copies[k, 6].wait_recv()
            go(k, block_rows(2), BLOCK, sibling, 10)

        def arrived(k):
            for number in (7, 8, 9, 10):
                copies[k, number].wait_recv()

        return [along_a, along_b, onward, last, arrived]

    def run(stages, skew):
        tasks = [(s + skew * k, -s, k) for s in range(len(stages)) for k in range(CHUNKS)]
        for _, s, k in sorted(tasks):
            stages[-s](k)

    token_lanes = [
        pl.ds(0, LANES + cols) if k == 0 else pl.ds(LANES + k * cols, cols) for k in range(CHUNKS)
    ]

    def project(k):
        def step(i):
            r = pl.ds(pl.multiple_of(i * 256, 256), 256)
            part = trows[r, LANES + k * cols : LANES + (k + 1) * cols]
            depth = slice(k * cols, (k + 1) * cols)
            gate = dot(part, gate_w[depth, :])
            up = dot(part, up_w[depth, :])
            pre = dot(part, enc_w[depth, :])
            if k > 0:
                gate += acc_gate[r, :]
                up += acc_up[r, :]
                pre += acc_pre[r, :]
            acc_gate[r, :] = gate
            acc_up[r, :] = up
            acc_pre[r, :] = pre

        each(ROWS // 256, step)

    stages = gather_stages(trows, token_lanes, 0)
    for k in range(CHUNKS):
        stages[0](k)

    loads[1].wait()

    def split_dec(i):
        r = pl.ds(pl.multiple_of(i * 16, 16), 16)
        high, low = split(dec_stage[r, :])
        dec_w[r, :] = high
        dec_w[pl.ds(pl.multiple_of(features + i * 16, 16), 16), :] = low
        dec_w[pl.ds(pl.multiple_of(2 * features + i * 16, 16), 16), :] = high

    each(features // 16, split_dec)
    for load in loads[2:]:
        load.wait()
    filled = 3 * features + hidden_width
    dec_w[filled : dec_w.shape[0], :] = jnp.zeros((dec_w.shape[0] - filled, width), bf16)
    left[:, 3 * features + hidden_width - hidden_width % LANES : left.shape[1]] = jnp.zeros(
        (ROWS, left.shape[1] - 3 * features - hidden_width + hidden_width % LANES), bf16
    )
    run(stages[1:] + [project], 1)

    rows_copy = pltpu.make_async_copy(trows.at[:, pl.ds(LANES, width)], rows_out, local_sem.at[5])
    rows_copy.start()

    threshold = jnp.exp(log_threshold[...])

    def activate(i):
        r = pl.ds(pl.multiple_of(i * 64, 64), 64)
        gate = acc_gate[r, :]
        hidden = (gate / (1.0 + jnp.exp(-gate)) * acc_up[r, :]).astype(bf16)
        left[r, 3 * features : 3 * features + hidden_width] = -hidden
        preact = acc_pre[r, 0:features] + acc_pre[r, features : 2 * features] + bias[...]
        shifted = preact - threshold
        soft_gate = 1.0 / (1.0 + jnp.exp(-shifted / sharpness))
        active = preact * soft_gate
        gate_s[r, :] = soft_gate
        shift_s[r, :] = shifted
        high, low = split(active)
        left[r, 0:features] = high
        left[r, features : 2 * features] = high
        left[r, 2 * features : 3 * features] = low
        acc_grad[r, :] = active

    each(ROWS // 64, activate)

    base = 11
    copies = {}

    def reconstruct(k):
        tile = 512

        def mul(start, out):
            def step(n):
                at = pl.ds(pl.multiple_of(k * cols + n * tile, tile), tile)
                out[:, pl.ds(pl.multiple_of(n * tile, tile), tile)] = dot(left[al(start, HALF), :], dec_w[:, at])

            each(cols // tile, step)

        mul((1 - core) * HALF, psib)

        def code(i):
            r = pl.ds(pl.multiple_of(i * 16, 16), 16)
            encode(psib[r, :], sib_out.at[k], r)

        each(HALF // 16, code)
        copies[k, 0] = remote(sib_out.at[k], sib_in.at[k], sibling, k, base)
        mul(core * HALF, pown.at[k])

    def own_rows(k, start):
        return al(lax.rem(b + k, 4) * BLOCK + start, UNIT)

    def code_rows(k, shift, start, count, out, at, extra=None):
        def step(i):
            value = pown[k, own_rows(shift, start + i * UNIT), :]
            if extra is not None:
                value += decode(extra, al(i * UNIT, UNIT))
            encode(value, out, al(at + i * UNIT, UNIT))

        each(count // UNIT, step)

    half = BLOCK // 2

    def sum_cores(k):
        copies[k, 0].wait_recv()

        def step(i):
            r = pl.ds(pl.multiple_of(i * 16, 16), 16)
            pown[k, r, :] += decode(sib_in.at[k], r)

        each(HALF // 16, step)
        code_rows(k, 2, 0, half, b1_out.at[k, 0], 0)
        code_rows(k, 1, half, half, b1_out.at[k, 0], half)
        copies[k, 1] = remote(b1_out.at[k, 0], b1_in.at[k, 0], b_peer(1), k, base + 1)
        code_rows(k, 2, half, half, b1_out.at[k, 1], 0)
        code_rows(k, 3, 0, half, b1_out.at[k, 1], half)
        copies[k, 2] = remote(b1_out.at[k, 1], b1_in.at[k, 1], b_peer(3), k, base + 2)

    def pass_on(k):
        copies[k, 1].wait_recv()
        code_rows(k, 1, 0, half, b2_out.at[k, 0], 0, b1_in.at[k, 0])
        copies[k, 3] = remote(b2_out.at[k, 0], b2_in.at[k, 0], b_peer(1), k, base + 3)
        copies[k, 2].wait_recv()
        code_rows(k, 3, half, half, b2_out.at[k, 1], 0, b1_in.at[k, 1])
        copies[k, 4] = remote(b2_out.at[k, 1], b2_in.at[k, 1], b_peer(3), k, base + 4)

    def sum_b(k):
        copies[k, 3].wait_recv()
        copies[k, 4].wait_recv()

        def step(i):
            r = al(i * UNIT, UNIT)
            far = al(half + i * UNIT, UNIT)
            pown[k, own_rows(0, i * UNIT), :] += decode(b2_in.at[k, 0], r) + decode(b1_in.at[k, 1], far)
            pown[k, own_rows(0, half + i * UNIT), :] += decode(b2_in.at[k, 1], r) + decode(b1_in.at[k, 0], far)

        each(half // UNIT, step)
        for i in (1, 2, 3):
            target = lax.rem(a + i, 4) * UNIT
            encode(pown[k, own_rows(0, target), :], a_out.at[k, i - 1], pl.ds(0, UNIT))
            copies[k, 4 + i] = remote(a_out.at[k, i - 1], a_in.at[k, i - 1], a_peer(i), k, base + 4 + i)

    def sum_a(k):
        r = pl.ds(0, UNIT)
        value = pown[k, own_rows(0, a * UNIT), :]
        for i in (1, 2, 3):
            copies[k, 4 + i].wait_recv()
            value += decode(a_in.at[k, i - 1], r)
        pown[k, own_rows(0, a * UNIT), :] = value
        encode(value, y_out.at[k], r)
        copies[k, 8] = remote(y_out.at[k], y_in.at[k], partner, k, base + 8)

    grad_lanes = [pl.ds(k * cols, cols) for k in range(CHUNKS)]
    grad_stages = gather_stages(rgrad, grad_lanes, 20)

    def sum_y(k):
        copies[k, 8].wait_recv()
        value = pown[k, own_rows(0, a * UNIT), :] + decode(y_in.at[k], pl.ds(0, UNIT))
        weight = trows[al(own_unit, UNIT), 0:LANES].astype(f32)[:, 0:1]
        rgrad[al(own_unit, UNIT), k * cols : (k + 1) * cols] = (2.0 * weight * value).astype(bf16)
        grad_stages[0](k)

    grad_copies = []
    act_part = acc_pre

    def back(k):
        grad_copy = pltpu.make_async_copy(
            rgrad.at[:, pl.ds(k * cols, cols)], grad_out.at[:, pl.ds(k * cols, cols)], local_sem.at[6 + k]
        )
        grad_copy.start()
        grad_copies.append(grad_copy)

        def step(i):
            r = pl.ds(pl.multiple_of(i * 256, 256), 256)
            at = slice(k * cols, (k + 1) * cols)
            part = dot_nt(rgrad[r, at], dec_w[0 : 2 * features, at])
            if k > 0:
                part += act_part[r, :]
            act_part[r, :] = part

        each(ROWS // 256, step)

    def transpose_active(i):
        r = pl.ds(pl.multiple_of(i * 128, 128), 128)
        high, low = split(acc_grad[r, :].T)
        act_high_out[:, r] = high
        act_low_out[:, r] = low

    def start_sums(k):
        reconstruct(k)
        if k == CHUNKS - 1:
            each(ROWS // 128, transpose_active)

    run([start_sums, sum_cores, pass_on, sum_b, sum_a, sum_y] + grad_stages[1:] + [back], 1)

    def finish(i, carry):
        bias_sum, slope_sum = carry
        r = pl.ds(pl.multiple_of(i * 64, 64), 64)
        grad_active = act_part[r, 0:features] + act_part[r, features : 2 * features]
        grad_pre = grad_active * gate_s[r, :]
        pre_high_out[r, :], pre_low_out[r, :] = split(grad_pre)
        hat = jnp.maximum(0.0, 1.0 - jnp.abs(shift_s[r, :]) / kernel_width) / kernel_width
        weight = trows[r, 0:LANES].astype(f32)[:, 0:1]
        slope = (grad_active * threshold + density_weight * weight) * hat
        return (
            bias_sum + jnp.sum(grad_pre, axis=0, keepdims=True),
            slope_sum + jnp.sum(slope, axis=0, keepdims=True),
        )

    zero = jnp.zeros((1, features), f32)
    bias_sum, slope_sum = lax.fori_loop(0, ROWS // 64, finish, (zero, zero))
    bias_out[...] = bias_sum
    threshold_out[...] = -threshold * slope_sum

    rows_copy.wait()
    for copy in grad_copies:
        copy.wait()
    for copy in sends:
        copy.wait_send()


def gradient_kernel(rows, grad, act_high, act_low, pre_high, pre_low, enc_out, dec_out):
    dec_out[...] = dot(act_high[...], grad[...]) + dot(act_low[...], grad[...])
    enc_out[...] = dot_tn(rows[...], pre_high[...]) + dot_tn(rows[...], pre_low[...])


def body(
    tokens,
    expert_ids,
    route_weights,
    gate_proj,
    up_proj,
    down_proj,
    enc_weight,
    enc_bias,
    log_threshold,
    dec_weight,
):
    width = tokens.shape[1]
    hidden = gate_proj.shape[1]
    features = enc_weight.shape[1]
    cols = width // CHUNKS
    depth = 3 * features + (hidden + LANES - 1) // LANES * LANES
    vmem = pl.BlockSpec(memory_space=pltpu.VMEM)
    hbm = pl.BlockSpec(memory_space=pl.ANY)
    shape = jax.ShapeDtypeStruct
    coded = jnp.int16
    message = cols + LANES
    outs = pl.pallas_call(
        forward_kernel,
        name="forward",
        out_shape=(
            shape((ROWS, width), bf16),
            shape((ROWS, width), bf16),
            shape((features, ROWS), bf16),
            shape((features, ROWS), bf16),
            shape((ROWS, features), bf16),
            shape((ROWS, features), bf16),
            shape((1, features), f32),
            shape((1, features), f32),
        ),
        in_specs=[vmem] * 5 + [hbm] * 5,
        out_specs=(hbm, hbm) + (vmem,) * 6,
        scratch_shapes=[
            pltpu.VMEM((width, features), f32),
            pltpu.VMEM((features, width), f32),
            pltpu.VMEM((width, hidden), bf16),
            pltpu.VMEM((width, hidden), bf16),
            pltpu.VMEM((width, 2 * features), bf16),
            pltpu.VMEM((depth, width), bf16),
            pltpu.VMEM((UNIT, width // 4 + LANES), f32),
            pltpu.VMEM((2, UNIT, width // 4 + LANES), bf16),
            pltpu.VMEM((4, UNIT, width // 4 + LANES), bf16),
            pltpu.VMEM((UNIT, width + LANES), f32),
            pltpu.VMEM((ROWS, width + LANES), bf16),
            pltpu.VMEM((ROWS, width), bf16),
            pltpu.VMEM((ROWS, hidden), f32),
            pltpu.VMEM((ROWS, hidden), f32),
            pltpu.VMEM((ROWS, 2 * features), f32),
            pltpu.VMEM((ROWS, depth), bf16),
            pltpu.VMEM((ROWS, features), f32),
            pltpu.VMEM((ROWS, features), f32),
            pltpu.VMEM((ROWS, features), f32),
            pltpu.VMEM((HALF, cols), f32),
            pltpu.VMEM((CHUNKS, HALF, cols), f32),
            pltpu.VMEM((CHUNKS, HALF, message), coded),
            pltpu.VMEM((CHUNKS, HALF, message), coded),
            pltpu.VMEM((CHUNKS, 2, BLOCK, message), coded),
            pltpu.VMEM((CHUNKS, 2, BLOCK, message), coded),
            pltpu.VMEM((CHUNKS, 2, BLOCK // 2, message), coded),
            pltpu.VMEM((CHUNKS, 2, BLOCK // 2, message), coded),
            pltpu.VMEM((CHUNKS, 3, UNIT, message), coded),
            pltpu.VMEM((CHUNKS, 3, UNIT, message), coded),
            pltpu.VMEM((CHUNKS, UNIT, message), coded),
            pltpu.VMEM((CHUNKS, UNIT, message), coded),
            pltpu.SemaphoreType.DMA((CHUNKS, 31)),
            pltpu.SemaphoreType.DMA((CHUNKS, 31)),
            pltpu.SemaphoreType.DMA((3,)),
            pltpu.SemaphoreType.DMA((3,)),
            pltpu.SemaphoreType.DMA((6 + CHUNKS,)),
        ],
        compiler_params=pltpu.CompilerParams(
            collective_id=0, has_side_effects=True, vmem_limit_bytes=60 * 1024 * 1024
        ),
    )(
        tokens,
        expert_ids,
        route_weights,
        enc_bias.reshape(1, -1),
        log_threshold.reshape(1, -1),
        gate_proj,
        up_proj,
        down_proj,
        enc_weight,
        dec_weight,
    )
    rows, grad, act_high, act_low, pre_high, pre_low, grad_bias, grad_threshold = outs
    tile = 512
    whole = lambda i: (0, 0)
    grad_encoder, grad_decoder = pl.pallas_call(
        gradient_kernel,
        name="gradients",
        grid=(width // tile,),
        out_shape=(shape((width, features), f32), shape((features, width), f32)),
        in_specs=[
            pl.BlockSpec((ROWS, tile), lambda i: (0, i)),
            pl.BlockSpec((ROWS, tile), lambda i: (0, i)),
            pl.BlockSpec((features, ROWS), whole),
            pl.BlockSpec((features, ROWS), whole),
            pl.BlockSpec((ROWS, features), whole),
            pl.BlockSpec((ROWS, features), whole),
        ],
        out_specs=(
            pl.BlockSpec((tile, features), lambda i: (i, 0)),
            pl.BlockSpec((features, tile), lambda i: (0, i)),
        ),
        compiler_params=pltpu.CompilerParams(vmem_limit_bytes=32 * 1024 * 1024),
    )(rows, grad, act_high, act_low, pre_high, pre_low)
    return (grad_encoder, grad_decoder, grad_bias.reshape(-1), grad_threshold.reshape(-1))


def solution(mesh):
    in_specs = (
        P(("expert", "feat"), None),
        P(("expert", "feat"), None),
        P(("expert", "feat"), None),
        P(None, ("expert", "feat")),
        P(None, ("expert", "feat")),
        P(("expert", "feat"), None),
        P(None, ("expert", "feat")),
        P(("expert", "feat")),
        P(("expert", "feat")),
        P(("expert", "feat"), None),
    )
    out_specs = (
        P(None, ("expert", "feat")),
        P(("expert", "feat"), None),
        P(("expert", "feat")),
        P(("expert", "feat")),
    )
    return jax.shard_map(body, mesh=mesh, in_specs=in_specs, out_specs=out_specs, check_vma=False)
```

time: 475 us -> 127 us (0.27)
  blocking collectives: 218 us -> 0 us
  waiting for transfers between devices: 168 us -> 0 us
  Pallas kernels: 0 us -> 107 us
  matrix products: 63.9 us -> 0 us
  between operations: 14.1 us -> 0.67 us
  local copies, waits for them, and re-layouts: 7.86 us -> 18.5 us
    all_to_all x2 -> x0, blocking collectives: 192 us -> none  [the longest x1 182 us: body(): lax.all_to_all(send_weights, 'expert', split_axis=0, concat_axis=0, tiled...]
    psum x1 -> x0, waiting for transfers between devices: 120 us -> none  [body(): feat_total = lax.psum(partial_error, 'feat')]
    pallas_call x0 -> x2, Pallas kernels: none -> 107 us  [the longest x1 100 us: body(): pl.pallas_call(forward_kernel, name='forward', out_shape=(shape((ROWS, wi...]
    dot_general x8 -> x0, matrix products: 63.9 us -> none  [the longest x2 17.8 us: contract_rows(): lax.dot_general(left, right, (((0,), (0,)), ((), ())), precision=highest)]
    all_gather x1 -> x0, waiting for transfers between devices: 48 us -> none  [body(): lax.all_gather(came_rows, 'feat', axis=0, tiled=True)]
    all_gather x1 -> x0, blocking collectives: 26.1 us -> none  [body(): lax.all_gather(came_weights, 'feat', axis=0, tiled=True)]
    unnamed x16 -> x24, local copies, waits for them, and re-layouts: 0.04 us -> 18.5 us
    reshape x1 -> x0, local copies, waits for them, and re-layouts: 6.87 us -> none  [body(): token_rows = all_rows.reshape(-1, width)]
  transfers between devices with their start and end apart: 3 -> 0, of which waited for: 2 -> 0; matrix products, arithmetic and copies ran while one was open for 0% -> 0% of each run, Pallas kernels for 0% -> 0%
where the time goes in v2:
time: 127 us; the launch traced here: 126 us
  Pallas kernels  107 us (84%)
  local copies, waits for them, and re-layouts  18.5 us (15%)
    pallas_call x1, Pallas kernels, body(): pl.pallas_call(forward_kernel, name='forward', out_shape=(shape((ROWS, wi...  100 us
    unnamed x24, local copies, waits for them, and re-layouts  18.5 us
    pallas_call x1, Pallas kernels, body(): pl.pallas_call(gradient_kernel, name='gradients', grid=(width // tile,),...  7.23 us

profile of v2, /device:TPU:1, one launch (start us, length us, event | category | flops | bytes accessed | tf_op | source)
XLA Modules:
  0.0 126.4 jit_solution(11936534154550059141)
XLA Ops:
  0.6 0.0 copy-start.6
  0.6 1.5 %copy.15.weights = bf16[8,2]{1,0:T(8,128)(2,1)} copy(bf16[8,2]{0,1:T(2,128)(2,1)} %param.12) | data formatting | bytes 64 | tf_op args[2]
  2.1 1.3 %copy.14.ids = s32[8,2]{1,0:T(8,128)} copy(s32[8,2]{0,1:T(2,128)} %param.11) | data formatting | bytes 128 | tf_op args[1]
  3.5 4.0 %copy.16.gate_hbm = bf16[4096,224]{1,0:T(8,128)(2,1)} copy(bf16[4096,224]{0,1:T(8,128)(2,1)} %param.13) | data formatting | bytes 3670016 | tf_op args[3]
  7.4 0.0 copy-done.6
  7.4 2.4 %copy.17.up_hbm = bf16[4096,224]{1,0:T(8,128)(2,1)} copy(bf16[4096,224]{0,1:T(8,128)(2,1)S(1)} %copy-done.6) | data formatting | bytes 3670016 | tf_op args[4]
  9.9 100.0 %forward.1 = (bf16[512,4096]{1,0:T(8,128)(2,1)}, bf16[512,4096]{1,0:T(8,128)(2,1)}, bf16[256,512]{1,0:T(8,128)(2,1)}, bf16[256,512]{1,0:T(8,128)(2,1)}, bf16[512...) custom-call(bf16[8,4096]{1,0:T(8,128)(2,1)} %tokens.1, s32[8,2]{1,0:T(8,128)} %copy.14.ids, ...), custom_call_target="tpu_custom_call" | custom-call | tf_op jit(solution)/shard_map/forward/pallas_call | solution.py:541
  109.9 0.0 copy-start
  109.9 2.2 %copy-done = bf16[512,4096]{1,0:T(8,128)(2,1)S(1)} copy-done((bf16[512,4096]{1,0:T(8,128)(2,1)S(1)}, bf16[512,4096]{1,0:T(8,128)(2,1)}, u32[]{:S(2)}) %copy-start) | copy-done | bytes 4194328
  112.0 0.0 copy-start.1
  112.0 2.2 %copy-done.1 = bf16[512,4096]{1,0:T(8,128)(2,1)S(1)} copy-done((bf16[512,4096]{1,0:T(8,128)(2,1)S(1)}, bf16[512,4096]{1,0:T(8,128)(2,1)}, u32[]{:S(2)}) %copy-start.1) | copy-done | bytes 4194328
  114.2 0.9 copy-done.2
  115.2 0.0 copy-start.3
  115.2 0.9 copy-done.3
  116.1 0.0 copy-start.4
  116.1 0.9 copy-done.4
  117.1 0.0 copy-start.5
  117.1 0.9 copy-done.5
  118.0 0.0 copy-start.8
  118.0 7.2 %gradients.1 = (f32[4096,256]{1,0:T(8,128)}, f32[256,4096]{1,0:T(8,128)}) custom-call(bf16[512,4096]{1,0:T(8,128)(2,1)S(1)} %copy-done, bf16[512,4096]{1,0:T(8,128)(2,1)S(1)} %copy-done.1, bf16[256,512]{1,0:T(8,128)(2,1)S(1)} %copy-done.2, bf16[256,512]{1,0:T(8,128)(2,1)S(1)} %copy-done.3, bf16[512,256]{1,0:T(8,128)(2,1)S(1)} %copy-done.4, ...), custom_call_target="tpu_custom_call" | custom-call | tf_op jit(solution)/shard_map/gradients/pallas_call | solution.py:612
  125.3 0.0 copy-done.8
  125.3 0.6 copy.20
  125.8 0.0 copy-done.7
  125.8 0.6 copy.21
  (2 shorter events, 0.0 us)
Async XLA Ops:
  0.6 6.8 %copy-start.6 = (bf16[4096,224]{0,1:T(8,128)(2,1)S(1)}, bf16[4096,224]{0,1:T(8,128)(2,1)}, u32[]{:S(2)}) copy-start(bf16[4096,224]{0,1:T(8,128)(2,1)} %param.14) | copy-start | bytes 5505028
  109.9 2.2 %copy-start = (bf16[512,4096]{1,0:T(8,128)(2,1)S(1)}, bf16[512,4096]{1,0:T(8,128)(2,1)}, u32[]{:S(2)}) copy-start(bf16[512,4096]{1,0:T(8,128)(2,1)} %get-tuple-element.14.rows) | copy-start | bytes 12582916
  112.0 2.2 %copy-start.1 = (bf16[512,4096]{1,0:T(8,128)(2,1)S(1)}, bf16[512,4096]{1,0:T(8,128)(2,1)}, u32[]{:S(2)}) copy-start(bf16[512,4096]{1,0:T(8,128)(2,1)} %get-tuple-element.15.grad) | copy-start | bytes 12582916
  114.2 0.9 copy-start.2
  115.2 0.9 copy-start.3
  116.1 0.9 copy-start.4
  117.1 0.9 copy-start.5
  118.0 7.2 %copy-start.8 = (f32[1,256]{1,0:T(1,128)S(1)}, f32[1,256]{1,0:T(1,128)}, u32[]{:S(2)}) copy-start(f32[1,256]{1,0:T(1,128)} %get-tuple-element.22) | copy-start | bytes 3076
  118.0 7.8 %copy-start.7 = (f32[1,256]{1,0:T(1,128)S(1)}, f32[1,256]{1,0:T(1,128)}, u32[]{:S(2)}) copy-start(f32[1,256]{1,0:T(1,128)} %get-tuple-element.23) | copy-start | bytes 3076

commit v3 on v2

--- a/solution.py
+++ b/solution.py
@@ -15,7 +15,9 @@
 kernel_width = 0.5
 density_weight = 0.01
 
-CHUNKS = 2
+CHUNKS = 4
+GATHER_SPACING = 0.9
+SUM_SPACING = 1.0
 LANES = 128
 UNIT = 16
 BLOCK = 4 * UNIT
@@ -40,19 +42,31 @@
     return high, (value - high.astype(f32)).astype(bf16)
 
 
-def encode(value, out, rows):
+def widest(value, so_far):
+    for at in range(0, value.shape[1], LANES):
+        so_far = jnp.maximum(so_far, jnp.abs(value[:, at : at + LANES]))
+    return so_far
+
+
+def exponent(so_far):
+    largest = jnp.max(so_far, axis=(0, 1), keepdims=True)
+    return jnp.broadcast_to(jnp.ceil(jnp.log2(jnp.maximum(largest, 1e-30))), so_far.shape)
+
+
+def over(tile, width):
+    return jnp.concatenate([tile] * (width // LANES), axis=1)
+
+
+def encode(value, power, out, rows):
     width = value.shape[1]
-    largest = jnp.max(jnp.abs(value), axis=1, keepdims=True)
-    power = jnp.ceil(jnp.log2(jnp.maximum(largest, 1e-30)))
-    out[rows, 0:width] = jnp.round(value * jnp.exp2(14.0 - power)).astype(jnp.int32).astype(jnp.int16)
-    lanes = jnp.broadcast_to(power.astype(jnp.int32), (value.shape[0], LANES))
-    out[rows, width : width + LANES] = lanes.astype(jnp.int16)
+    out[rows, 0:width] = jnp.round(value * over(jnp.exp2(14.0 - power), width)).astype(jnp.int32).astype(jnp.int16)
+    out[rows, width : width + LANES] = power.astype(jnp.int32).astype(jnp.int16)
 
 
 def decode(ref, rows):
     width = ref.shape[1] - LANES
-    power = ref[rows, width : width + LANES].astype(jnp.int32).astype(f32)[:, 0:1]
-    return ref[rows, 0:width].astype(jnp.int32).astype(f32) * jnp.exp2(power - 14.0)
+    scale = jnp.exp2(ref[rows, width : width + LANES].astype(jnp.int32).astype(f32) - 14.0)
+    return ref[rows, 0:width].astype(jnp.int32).astype(f32) * over(scale, width)
 
 
 def each(count, step):
@@ -75,11 +89,8 @@
     enc_hbm,
     dec_hbm,
     rows_out,
-    grad_out,
-    act_high_out,
-    act_low_out,
-    pre_high_out,
-    pre_low_out,
+    dec_out,
+    pre_out,
     bias_out,
     threshold_out,
     enc_stage,
@@ -94,6 +105,7 @@
     unit32,
     trows,
     rgrad,
+    act_s,
     acc_gate,
     acc_up,
     acc_pre,
@@ -121,7 +133,7 @@
 ):
     width = tokens.shape[1]
     cols = width // CHUNKS
-    hidden_width = gate_w.shape[1]
+    hidden_width = gate_w.shape[0]
     features = enc_w.shape[1] // 2
     piece = width // 4
 
@@ -172,10 +184,15 @@
     row_id = lax.broadcasted_iota(jnp.int32, (8, 1), 0)
     values = tokens[...].astype(f32)
     route = weights[...].astype(f32)
+    diagonal = row_id == lax.broadcasted_iota(jnp.int32, (8, 8), 1)
+
+    def upright(row):
+        return jnp.sum(jnp.where(diagonal, jnp.broadcast_to(row, (8, 8)), 0.0), axis=1, keepdims=True)
+
     for expert in range(2):
         match = ids[...] == expert
-        named = jnp.sum(jnp.where(match, 1.0, 0.0), axis=1, keepdims=True)
-        weight = jnp.sum(jnp.where(match, route, 0.0), axis=1, keepdims=True)
+        named = upright(jnp.sum(jnp.where(match, 1.0, 0.0), axis=0, keepdims=True))
+        weight = upright(jnp.sum(jnp.where(match, route, 0.0), axis=0, keepdims=True))
         slot = jnp.zeros((8, 1), f32)
         for t in range(7):
             slot += jnp.where(row_id > t, named[t : t + 1, :], 0.0)
@@ -282,32 +299,28 @@
 
         return [along_a, along_b, onward, last, arrived]
 
-    def run(stages, skew):
-        tasks = [(s + skew * k, -s, k) for s in range(len(stages)) for k in range(CHUNKS)]
-        for _, s, k in sorted(tasks):
-            stages[-s](k)
+    def run(stages, spacing):
+        tasks = [(at + spacing * k, -at, k, stage) for at, stage in stages for k in range(CHUNKS)]
+        for _, _, k, stage in sorted(tasks, key=lambda task: task[:3]):
+            stage(k)
 
     token_lanes = [
         pl.ds(0, LANES + cols) if k == 0 else pl.ds(LANES + k * cols, cols) for k in range(CHUNKS)
     ]
 
     def project(k):
-        def step(i):
-            r = pl.ds(pl.multiple_of(i * 256, 256), 256)
-            part = trows[r, LANES + k * cols : LANES + (k + 1) * cols]
-            depth = slice(k * cols, (k + 1) * cols)
-            gate = dot(part, gate_w[depth, :])
-            up = dot(part, up_w[depth, :])
-            pre = dot(part, enc_w[depth, :])
-            if k > 0:
-                gate += acc_gate[r, :]
-                up += acc_up[r, :]
-                pre += acc_pre[r, :]
-            acc_gate[r, :] = gate
-            acc_up[r, :] = up
-            acc_pre[r, :] = pre
-
-        each(ROWS // 256, step)
+        part = trows[:, LANES + k * cols : LANES + (k + 1) * cols]
+        depth = slice(k * cols, (k + 1) * cols)
+        gate = dot_nt(part, gate_w[:, depth])
+        up = dot_nt(part, up_w[:, depth])
+        pre = dot(part, enc_w[depth, :])
+        if k > 0:
+            gate += acc_gate[...]
+            up += acc_up[...]
+            pre += acc_pre[...]
+        acc_gate[...] = gate
+        acc_up[...] = up
+        acc_pre[...] = pre
 
     stages = gather_stages(trows, token_lanes, 0)
     for k in range(CHUNKS):
@@ -330,7 +343,11 @@
     left[:, 3 * features + hidden_width - hidden_width % LANES : left.shape[1]] = jnp.zeros(
         (ROWS, left.shape[1] - 3 * features - hidden_width + hidden_width % LANES), bf16
     )
-    run(stages[1:] + [project], 1)
+    def finish_rows(k):
+        stages[4](k)
+        project(k)
+
+    run([(0, stages[1]), (4.0, stages[2]), (7.0, stages[3]), (9.0, finish_rows)], GATHER_SPACING)
 
     rows_copy = pltpu.make_async_copy(trows.at[:, pl.ds(LANES, width)], rows_out, local_sem.at[5])
     rows_copy.start()
@@ -359,35 +376,49 @@
     base = 11
     copies = {}
 
-    def reconstruct(k):
-        tile = 512
-
-        def mul(start, out):
-            def step(n):
-                at = pl.ds(pl.multiple_of(k * cols + n * tile, tile), tile)
-                out[:, pl.ds(pl.multiple_of(n * tile, tile), tile)] = dot(left[al(start, HALF), :], dec_w[:, at])
-
-            each(cols // tile, step)
-
-        mul((1 - core) * HALF, psib)
+    none = jnp.zeros((UNIT, LANES), f32)
+
+    def multiply(k, start, out):
+        tile = 1024
+
+        def step(n):
+            at = pl.ds(pl.multiple_of(k * cols + n * tile, tile), tile)
+            out[:, pl.ds(pl.multiple_of(n * tile, tile), tile)] = dot(left[al(start, HALF), :], dec_w[:, at])
+
+        each(cols // tile, step)
+
+    def for_sibling(k):
+        multiply(k, (1 - core) * HALF, psib)
+        power = exponent(
+            lax.fori_loop(0, HALF // UNIT, lambda i, m: widest(psib[al(i * UNIT, UNIT), :], m), none)
+        )
 
         def code(i):
-            r = pl.ds(pl.multiple_of(i * 16, 16), 16)
-            encode(psib[r, :], sib_out.at[k], r)
-
-        each(HALF // 16, code)
+            r = al(i * UNIT, UNIT)
+            encode(psib[r, :], power, sib_out.at[k], r)
+
+        each(HALF // UNIT, code)
         copies[k, 0] = remote(sib_out.at[k], sib_in.at[k], sibling, k, base)
-        mul(core * HALF, pown.at[k])
-
-    def own_rows(k, start):
-        return al(lax.rem(b + k, 4) * BLOCK + start, UNIT)
-
-    def code_rows(k, shift, start, count, out, at, extra=None):
+
+    def for_own(k):
+        multiply(k, core * HALF, pown.at[k])
+
+    def own_rows(shift, start):
+        return al(lax.rem(b + shift, 4) * BLOCK + start, UNIT)
+
+    def add(k, rows, count, came, so_far):
+        def step(i, m):
+            value = pown[k, rows(i), :]
+            for ref, at in came:
+                value += decode(ref, al(at + i * UNIT, UNIT))
+            pown[k, rows(i), :] = value
+            return widest(value, m)
+
+        return lax.fori_loop(0, count // UNIT, step, so_far)
+
+    def code_rows(k, shift, start, count, power, out, at):
         def step(i):
-            value = pown[k, own_rows(shift, start + i * UNIT), :]
-            if extra is not None:
-                value += decode(extra, al(i * UNIT, UNIT))
-            encode(value, out, al(at + i * UNIT, UNIT))
+            encode(pown[k, own_rows(shift, start + i * UNIT), :], power, out, al(at + i * UNIT, UNIT))
 
         each(count // UNIT, step)
 
@@ -395,51 +426,43 @@
 
     def sum_cores(k):
         copies[k, 0].wait_recv()
-
-        def step(i):
-            r = pl.ds(pl.multiple_of(i * 16, 16), 16)
-            pown[k, r, :] += decode(sib_in.at[k], r)
-
-        each(HALF // 16, step)
-        code_rows(k, 2, 0, half, b1_out.at[k, 0], 0)
-        code_rows(k, 1, half, half, b1_out.at[k, 0], half)
+        power = exponent(add(k, lambda i: al(i * UNIT, UNIT), HALF, [(sib_in.at[k], 0)], none))
+        code_rows(k, 2, 0, half, power, b1_out.at[k, 0], 0)
+        code_rows(k, 1, half, half, power, b1_out.at[k, 0], half)
         copies[k, 1] = remote(b1_out.at[k, 0], b1_in.at[k, 0], b_peer(1), k, base + 1)
-        code_rows(k, 2, half, half, b1_out.at[k, 1], 0)
-        code_rows(k, 3, 0, half, b1_out.at[k, 1], half)
+        code_rows(k, 2, half, half, power, b1_out.at[k, 1], 0)
+        code_rows(k, 3, 0, half, power, b1_out.at[k, 1], half)
         copies[k, 2] = remote(b1_out.at[k, 1], b1_in.at[k, 1], b_peer(3), k, base + 2)
 
     def pass_on(k):
         copies[k, 1].wait_recv()
-        code_rows(k, 1, 0, half, b2_out.at[k, 0], 0, b1_in.at[k, 0])
+        power = exponent(add(k, lambda i: own_rows(1, i * UNIT), half, [(b1_in.at[k, 0], 0)], none))
+        code_rows(k, 1, 0, half, power, b2_out.at[k, 0], 0)
         copies[k, 3] = remote(b2_out.at[k, 0], b2_in.at[k, 0], b_peer(1), k, base + 3)
         copies[k, 2].wait_recv()
-        code_rows(k, 3, half, half, b2_out.at[k, 1], 0, b1_in.at[k, 1])
+        power = exponent(add(k, lambda i: own_rows(3, half + i * UNIT), half, [(b1_in.at[k, 1], 0)], none))
+        code_rows(k, 3, half, half, power, b2_out.at[k, 1], 0)
         copies[k, 4] = remote(b2_out.at[k, 1], b2_in.at[k, 1], b_peer(3), k, base + 4)
 
     def sum_b(k):
         copies[k, 3].wait_recv()
         copies[k, 4].wait_recv()
-
-        def step(i):
-            r = al(i * UNIT, UNIT)
-            far = al(half + i * UNIT, UNIT)
-            pown[k, own_rows(0, i * UNIT), :] += decode(b2_in.at[k, 0], r) + decode(b1_in.at[k, 1], far)
-            pown[k, own_rows(0, half + i * UNIT), :] += decode(b2_in.at[k, 1], r) + decode(b1_in.at[k, 0], far)
-
-        each(half // UNIT, step)
+        largest = add(
+            k, lambda i: own_rows(0, i * UNIT), half, [(b2_in.at[k, 0], 0), (b1_in.at[k, 1], half)], none
+        )
+        largest = add(
+            k, lambda i: own_rows(0, half + i * UNIT), half, [(b2_in.at[k, 1], 0), (b1_in.at[k, 0], half)], largest
+        )
+        power = exponent(largest)
         for i in (1, 2, 3):
-            target = lax.rem(a + i, 4) * UNIT
-            encode(pown[k, own_rows(0, target), :], a_out.at[k, i - 1], pl.ds(0, UNIT))
+            code_rows(k, 0, lax.rem(a + i, 4) * UNIT, UNIT, power, a_out.at[k, i - 1], 0)
             copies[k, 4 + i] = remote(a_out.at[k, i - 1], a_in.at[k, i - 1], a_peer(i), k, base + 4 + i)
 
     def sum_a(k):
-        r = pl.ds(0, UNIT)
-        value = pown[k, own_rows(0, a * UNIT), :]
         for i in (1, 2, 3):
             copies[k, 4 + i].wait_recv()
-            value += decode(a_in.at[k, i - 1], r)
-        pown[k, own_rows(0, a * UNIT), :] = value
-        encode(value, y_out.at[k], r)
+        largest = add(k, lambda i: own_rows(0, a * UNIT), UNIT, [(a_in.at[k, i], 0) for i in range(3)], none)
+        code_rows(k, 0, a * UNIT, UNIT, exponent(largest), y_out.at[k], 0)
         copies[k, 8] = remote(y_out.at[k], y_in.at[k], partner, k, base + 8)
 
     grad_lanes = [pl.ds(k * cols, cols) for k in range(CHUNKS)]
@@ -447,50 +470,60 @@
 
     def sum_y(k):
         copies[k, 8].wait_recv()
-        value = pown[k, own_rows(0, a * UNIT), :] + decode(y_in.at[k], pl.ds(0, UNIT))
+        value = pown[k, own_rows(0, a * UNIT), :] + decode(y_in.at[k], al(0, UNIT))
         weight = trows[al(own_unit, UNIT), 0:LANES].astype(f32)[:, 0:1]
         rgrad[al(own_unit, UNIT), k * cols : (k + 1) * cols] = (2.0 * weight * value).astype(bf16)
         grad_stages[0](k)
 
-    grad_copies = []
+    dec_copies = []
     act_part = acc_pre
 
     def back(k):
-        grad_copy = pltpu.make_async_copy(
-            rgrad.at[:, pl.ds(k * cols, cols)], grad_out.at[:, pl.ds(k * cols, cols)], local_sem.at[6 + k]
-        )
-        grad_copy.start()
-        grad_copies.append(grad_copy)
-
-        def step(i):
-            r = pl.ds(pl.multiple_of(i * 256, 256), 256)
-            at = slice(k * cols, (k + 1) * cols)
-            part = dot_nt(rgrad[r, at], dec_w[0 : 2 * features, at])
-            if k > 0:
-                part += act_part[r, :]
-            act_part[r, :] = part
-
-        each(ROWS // 256, step)
+        at = slice(k * cols, (k + 1) * cols)
+        part = rgrad[:, at]
+        both = dot(act_s[...], part)
+        dec_stage[:, at] = both[0:features, :] + both[features : 2 * features, :]
+        chunk = pl.ds(k * cols, cols)
+        dec_copy = pltpu.make_async_copy(dec_stage.at[:, chunk], dec_out.at[:, chunk], local_sem.at[6 + k])
+        dec_copy.start()
+        dec_copies.append(dec_copy)
+        total = dot_nt(part, dec_w[0 : 2 * features, at])
+        if k > 0:
+            total += act_part[...]
+        act_part[...] = total
 
     def transpose_active(i):
         r = pl.ds(pl.multiple_of(i * 128, 128), 128)
-        high, low = split(acc_grad[r, :].T)
-        act_high_out[:, r] = high
-        act_low_out[:, r] = low
-
-    def start_sums(k):
-        reconstruct(k)
+        act_s[0:features, r], act_s[features : 2 * features, r] = split(acc_grad[r, :].T)
+
+    def last_sum(k):
         if k == CHUNKS - 1:
             each(ROWS // 128, transpose_active)
-
-    run([start_sums, sum_cores, pass_on, sum_b, sum_a, sum_y] + grad_stages[1:] + [back], 1)
+        pass_on(k)
+
+    run(
+        [
+            (0, for_sibling),
+            (0.7, for_own),
+            (3.0, sum_cores),
+            (6.7, last_sum),
+            (9.7, sum_b),
+            (12.7, sum_a),
+            (15.7, sum_y),
+            (18.7, grad_stages[1]),
+            (22.5, grad_stages[2]),
+            (25.5, grad_stages[3]),
+            (27.5, lambda k: (grad_stages[4](k), back(k))),
+        ],
+        SUM_SPACING,
+    )
 
     def finish(i, carry):
         bias_sum, slope_sum = carry
         r = pl.ds(pl.multiple_of(i * 64, 64), 64)
         grad_active = act_part[r, 0:features] + act_part[r, features : 2 * features]
         grad_pre = grad_active * gate_s[r, :]
-        pre_high_out[r, :], pre_low_out[r, :] = split(grad_pre)
+        pre_out[r, 0:features], pre_out[r, features : 2 * features] = split(grad_pre)
         hat = jnp.maximum(0.0, 1.0 - jnp.abs(shift_s[r, :]) / kernel_width) / kernel_width
         weight = trows[r, 0:LANES].astype(f32)[:, 0:1]
         slope = (grad_active * threshold + density_weight * weight) * hat
@@ -505,15 +538,19 @@
     threshold_out[...] = -threshold * slope_sum
 
     rows_copy.wait()
-    for copy in grad_copies:
+    for copy in dec_copies:
         copy.wait()
     for copy in sends:
         copy.wait_send()
 
 
-def gradient_kernel(rows, grad, act_high, act_low, pre_high, pre_low, enc_out, dec_out):
-    dec_out[...] = dot(act_high[...], grad[...]) + dot(act_low[...], grad[...])
-    enc_out[...] = dot_tn(rows[...], pre_high[...]) + dot_tn(rows[...], pre_low[...])
+def gradient_kernel(rows, dec, pre, bias, slope, enc_out, dec_out, bias_out, slope_out):
+    features = enc_out.shape[1]
+    bias_out[...] = bias[0, :]
+    slope_out[...] = slope[0, :]
+    dec_out[...] = dec[...]
+    both = dot_tn(rows[...], pre[...])
+    enc_out[...] = both[:, 0:features] + both[:, features : 2 * features]
 
 
 def body(
@@ -543,21 +580,18 @@
         name="forward",
         out_shape=(
             shape((ROWS, width), bf16),
-            shape((ROWS, width), bf16),
-            shape((features, ROWS), bf16),
-            shape((features, ROWS), bf16),
-            shape((ROWS, features), bf16),
-            shape((ROWS, features), bf16),
+            shape((features, width), f32),
+            shape((ROWS, 2 * features), bf16),
             shape((1, features), f32),
             shape((1, features), f32),
         ),
         in_specs=[vmem] * 5 + [hbm] * 5,
-        out_specs=(hbm, hbm) + (vmem,) * 6,
+        out_specs=(hbm, hbm) + (vmem,) * 3,
         scratch_shapes=[
             pltpu.VMEM((width, features), f32),
             pltpu.VMEM((features, width), f32),
-            pltpu.VMEM((width, hidden), bf16),
-            pltpu.VMEM((width, hidden), bf16),
+            pltpu.VMEM((hidden, width), bf16),
+            pltpu.VMEM((hidden, width), bf16),
             pltpu.VMEM((width, 2 * features), bf16),
             pltpu.VMEM((depth, width), bf16),
             pltpu.VMEM((UNIT, width // 4 + LANES), f32),
@@ -566,6 +600,7 @@
             pltpu.VMEM((UNIT, width + LANES), f32),
             pltpu.VMEM((ROWS, width + LANES), bf16),
             pltpu.VMEM((ROWS, width), bf16),
+            pltpu.VMEM((2 * features, ROWS), bf16),
             pltpu.VMEM((ROWS, hidden), f32),
             pltpu.VMEM((ROWS, hidden), f32),
             pltpu.VMEM((ROWS, 2 * features), f32),
@@ -596,39 +631,44 @@
         ),
     )(
         tokens,
-        expert_ids,
-        route_weights,
+        expert_ids.T,
+        route_weights.T,
         enc_bias.reshape(1, -1),
         log_threshold.reshape(1, -1),
-        gate_proj,
-        up_proj,
+        gate_proj.T,
+        up_proj.T,
         down_proj,
         enc_weight,
         dec_weight,
     )
-    rows, grad, act_high, act_low, pre_high, pre_low, grad_bias, grad_threshold = outs
-    tile = 512
+    rows, grad_decoder, pre, grad_bias, grad_threshold = outs
+    tile = 2048
     whole = lambda i: (0, 0)
-    grad_encoder, grad_decoder = pl.pallas_call(
+    return pl.pallas_call(
         gradient_kernel,
         name="gradients",
         grid=(width // tile,),
-        out_shape=(shape((width, features), f32), shape((features, width), f32)),
+        out_shape=(
+            shape((width, features), f32),
+            shape((features, width), f32),
+            shape((features,), f32),
+            shape((features,), f32),
+        ),
         in_specs=[
             pl.BlockSpec((ROWS, tile), lambda i: (0, i)),
-            pl.BlockSpec((ROWS, tile), lambda i: (0, i)),
-            pl.BlockSpec((features, ROWS), whole),
-            pl.BlockSpec((features, ROWS), whole),
-            pl.BlockSpec((ROWS, features), whole),
-            pl.BlockSpec((ROWS, features), whole),
+            pl.BlockSpec((features, tile), lambda i: (0, i)),
+            pl.BlockSpec((ROWS, 2 * features), whole),
+            pl.BlockSpec((1, features), whole),
+            pl.BlockSpec((1, features), whole),
         ],
         out_specs=(
             pl.BlockSpec((tile, features), lambda i: (i, 0)),
             pl.BlockSpec((features, tile), lambda i: (0, i)),
+            pl.BlockSpec((features,), lambda i: (0,)),
+            pl.BlockSpec((features,), lambda i: (0,)),
         ),
-        compiler_params=pltpu.CompilerParams(vmem_limit_bytes=32 * 1024 * 1024),
-    )(rows, grad, act_high, act_low, pre_high, pre_low)
-    return (grad_encoder, grad_decoder, grad_bias.reshape(-1), grad_threshold.reshape(-1))
+        compiler_params=pltpu.CompilerParams(vmem_limit_bytes=60 * 1024 * 1024),
+    )(rows, grad_decoder, pre, grad_bias, grad_threshold)
 
 
 def solution(mesh):

time: 127 us -> 93.2 us (0.73)
  local copies, waits for them, and re-layouts: 18.5 us -> 0 us
  Pallas kernels: 107 us -> 92.4 us
    unnamed x24 -> x0, local copies, waits for them, and re-layouts: 18.5 us -> none
    pallas_call x1, Pallas kernels: 100 us -> 85.4 us  [body(): pl.pallas_call(forward_kernel, name='forward', out_shape=(shape((ROWS, wi...]
where the time goes in v3:
time: 93.2 us; the launch traced here: 93 us
  Pallas kernels  92.4 us (99%)
    pallas_call x1, Pallas kernels, body(): pl.pallas_call(forward_kernel, name='forward', out_shape=(shape((ROWS, wi...  85.4 us
    pallas_call x1, Pallas kernels, body(): pl.pallas_call(gradient_kernel, name='gradients', grid=(width // tile,),...  7.02 us

profile of v3, /device:TPU:1, one launch (start us, length us, event | category | flops | bytes accessed | tf_op | source)
XLA Modules:
  0.0 93.0 jit_solution(16252560020433297370)
XLA Ops:
  0.6 85.4 %forward.1 = (bf16[512,4096]{1,0:T(8,128)(2,1)}, f32[256,4096]{1,0:T(8,128)}, bf16[512,512]{1,0:T(8,128)(2,1)}, f32[1,256]{1,0:T(1,128)}, f32[1,256]{1,0:T(1,128)}) custom-call(bf16[8,4096]{1,0:T(8,128)(2,1)} %tokens.1, s32[2,8]{1,0:T(2,128)} %bitcast.8, bf16[2,8]{1,0:T(2,128)(2,1)} %bitcast.11, f32[1,256]{1,0:T(1,128)} %bitcast.9, f32[1,256]{1,0:T(1,128)} %bitcast.10, ...), custom_call_target="tpu_custom_call" | custom-call | tf_op jit(solution)/shard_map/forward/pallas_call | solution.py:578
  86.0 7.0 %gradients.1 = (f32[4096,256]{1,0:T(8,128)}, f32[256,4096]{1,0:T(8,128)}, f32[256]{0:T(256)}, f32[256]{0:T(256)}) custom-call(bf16[512,4096]{1,0:T(8,128)(2,1)} %get-tuple-element.9.rows, f32[256,4096]{1,0:T(8,128)} %get-tuple-element.10.dec, bf16[512,512]{1,0:T(8,128)(2,1)} %get-tuple-element.11.pre, f32[1,256]{1,0:T(1,128)} %get-tuple-element.12.bias, ...), custom_call_target="tpu_custom_call" | custom-call | tf_op jit(solution)/shard_map/gradients/pallas_call | solution.py:647

commit v4 on v3

--- a/solution.py
+++ b/solution.py
@@ -270,21 +270,32 @@
             copies[k, number] = remote(part, part, peer, k, base + number)
 
         def along_a(k):
-            for i in (1, 2, 3):
+            for i in (1, 3, 2):
                 go(k, own_unit, UNIT, a_peer(i), i - 1)
 
+        def pass_unit(k, away, number):
+            start = block_rows(0) + lax.rem(a + away, 4) * UNIT
+            go(k, start, UNIT, b_peer(1), number)
+            go(k, start, UNIT, b_peer(3), number + 1)
+
         def along_b(k):
-            for i in (1, 2, 3):
-                copies[k, i - 1].wait_recv()
-            go(k, block_rows(0), BLOCK, b_peer(1), 3)
-            go(k, block_rows(0), BLOCK, b_peer(3), 4)
+            if lane_ranges is token_lanes and k >= 2:
+                for number in (3, 4, 11, 12, 13, 14, 15, 16):
+                    copies[k - 2, number].wait_send()
+                    sends[:] = [c for c in sends if c is not copies[k - 2, number]]
+            pass_unit(k, 0, 3)
+            for away, number in ((3, 11), (1, 13), (2, 15)):
+                copies[k, 3 - away].wait_recv()
+                pass_unit(k, away, number)
             go(k, block_rows(0), BLOCK, sibling, 7)
 
         def onward(k):
-            copies[k, 3].wait_recv()
+            for number in (3, 11, 13, 15):
+                copies[k, number].wait_recv()
             go(k, block_rows(3), BLOCK // 2, b_peer(1), 5)
             go(k, block_rows(3), BLOCK, sibling, 8)
-            copies[k, 4].wait_recv()
+            for number in (4, 12, 14, 16):
+                copies[k, number].wait_recv()
             go(k, block_rows(1) + BLOCK // 2, BLOCK // 2, b_peer(3), 6)
             go(k, block_rows(1), BLOCK, sibling, 9)
 
@@ -373,7 +384,7 @@
 
     each(ROWS // 64, activate)
 
-    base = 11
+    base = 17
     copies = {}
 
     none = jnp.zeros((UNIT, LANES), f32)
@@ -466,7 +477,7 @@
         copies[k, 8] = remote(y_out.at[k], y_in.at[k], partner, k, base + 8)
 
     grad_lanes = [pl.ds(k * cols, cols) for k in range(CHUNKS)]
-    grad_stages = gather_stages(rgrad, grad_lanes, 20)
+    grad_stages = gather_stages(rgrad, grad_lanes, 26)
 
     def sum_y(k):
         copies[k, 8].wait_recv()
@@ -620,8 +631,8 @@
             pltpu.VMEM((CHUNKS, 3, UNIT, message), coded),
             pltpu.VMEM((CHUNKS, UNIT, message), coded),
             pltpu.VMEM((CHUNKS, UNIT, message), coded),
-            pltpu.SemaphoreType.DMA((CHUNKS, 31)),
-            pltpu.SemaphoreType.DMA((CHUNKS, 31)),
+            pltpu.SemaphoreType.DMA((CHUNKS, 43)),
+            pltpu.SemaphoreType.DMA((CHUNKS, 43)),
             pltpu.SemaphoreType.DMA((3,)),
             pltpu.SemaphoreType.DMA((3,)),
             pltpu.SemaphoreType.DMA((6 + CHUNKS,)),

time: 93.2 us -> 92.2 us (0.989)
  Pallas kernels: 92.4 us -> 91.4 us
    pallas_call x1, Pallas kernels: 85.4 us -> 84.4 us  [body(): pl.pallas_call(forward_kernel, name='forward', out_shape=(shape((ROWS, wi...]
where the time goes in v4:
time: 92.2 us; the launch traced here: 92.1 us
  Pallas kernels  91.4 us (99%)
    pallas_call x1, Pallas kernels, body(): pl.pallas_call(forward_kernel, name='forward', out_shape=(shape((ROWS, wi...  84.4 us
    pallas_call x1, Pallas kernels, body(): pl.pallas_call(gradient_kernel, name='gradients', grid=(width // tile,),...  7.02 us

profile of v4, /device:TPU:1, one launch (start us, length us, event | category | flops | bytes accessed | tf_op | source)
XLA Modules:
  0.0 92.1 jit_solution(15981032587293782433)
XLA Ops:
  0.6 84.4 %forward.1 = (bf16[512,4096]{1,0:T(8,128)(2,1)}, f32[256,4096]{1,0:T(8,128)}, bf16[512,512]{1,0:T(8,128)(2,1)}, f32[1,256]{1,0:T(1,128)}, f32[1,256]{1,0:T(1,128)}) custom-call(bf16[8,4096]{1,0:T(8,128)(2,1)} %tokens.1, s32[2,8]{1,0:T(2,128)} %bitcast.8, bf16[2,8]{1,0:T(2,128)(2,1)} %bitcast.11, f32[1,256]{1,0:T(1,128)} %bitcast.9, f32[1,256]{1,0:T(1,128)} %bitcast.10, ...), custom_call_target="tpu_custom_call" | custom-call | tf_op jit(solution)/shard_map/forward/pallas_call | solution.py:589
  85.1 7.0 %gradients.1 = (f32[4096,256]{1,0:T(8,128)}, f32[256,4096]{1,0:T(8,128)}, f32[256]{0:T(256)}, f32[256]{0:T(256)}) custom-call(bf16[512,4096]{1,0:T(8,128)(2,1)} %get-tuple-element.9.rows, f32[256,4096]{1,0:T(8,128)} %get-tuple-element.10.dec, bf16[512,512]{1,0:T(8,128)(2,1)} %get-tuple-element.11.pre, f32[1,256]{1,0:T(1,128)} %get-tuple-element.12.bias, ...), custom_call_target="tpu_custom_call" | custom-call | tf_op jit(solution)/shard_map/gradients/pallas_call | solution.py:658
